TPU v7x, 32 devices: a whole 2x2x4 slice. The times are simulated.
32 devices in a mesh: grp: 8 (over z, y), tp: 4 (over x, core).
Axes of the slice: x: 2, y: 2, z: 4, core: 2. Of those that a mesh axis runs over, the one named last changes fastest.
Arguments:
- tokens: bfloat16 [8, 3136, 512], P(None, 'grp'), may hold values from -6 to 6
- grad_out: bfloat16 [8, 3136, 512], P(None, 'grp'), may hold values from -6 to 6
- ln1_gain: bfloat16 [512], P('grp'), may hold values from 0.5 to 1.5
- ln1_shift: bfloat16 [512], P('grp'), may hold values from -3 to 3
- w_qkv: bfloat16 [512, 3, 512], P('grp', None, 'tp'), may hold values from -0.25 to 0.25
- qkv_bias: bfloat16 [2, 512], P(None, 'tp'), may hold values from -3 to 3
- rel_table: bfloat16 [2535, 16], P(None, 'tp'), may hold values from -4 to 4
- w_proj: bfloat16 [512, 512], P('grp', 'tp'), may hold values from -2 to 2
- proj_bias: bfloat16 [512], P('grp'), may hold values from -3 to 3
- ln2_gain: bfloat16 [512], P('grp'), may hold values from 0.5 to 1.5
- ln2_shift: bfloat16 [512], P('grp'), may hold values from -3 to 3
- w_in: bfloat16 [512, 2048], P('grp', 'tp'), may hold values from -0.25 to 0.25
- in_bias: bfloat16 [2048], P('tp'), may hold values from -3 to 3
- w_out: bfloat16 [512, 2048], P('grp', 'tp'), may hold values from -0.125 to 0.125
- out_bias: bfloat16 [512], P('grp'), may hold values from -3 to 3
Outputs:
- output: bfloat16 [8, 3136, 512], P(None, 'grp')
- grad_tokens: float32 [8, 3136, 512], P(None, 'grp')
- grad_ln1_gain: float32 [512], P('grp')
- grad_ln1_shift: float32 [512], P('grp')
- grad_w_qkv: float32 [512, 3, 512], P('grp', None, 'tp')
- grad_qkv_bias: float32 [2, 512], P(None, 'tp')
- grad_rel_table: float32 [2535, 16], P(None, 'tp')
- grad_w_proj: float32 [512, 512], P('grp', 'tp')
- grad_proj_bias: float32 [512], P('grp')
- grad_ln2_gain: float32 [512], P('grp')
- grad_ln2_shift: float32 [512], P('grp')
- grad_w_in: float32 [512, 2048], P('grp', 'tp')
- grad_in_bias: float32 [2048], P('tp')
- grad_w_out: float32 [512, 2048], P('grp', 'tp')
- grad_out_bias: float32 [512], P('grp')
All inputs are finite; a program needn't handle non-finite values.
Results may differ from a plain program's by a relative error of at most 0.011.
Values may be sent and summed in bfloat16 or wider, within the bound.
No kernel may reach another device: no remote copies, remote signals or barrier semaphores. Data moves between devices by JAX's collectives and lax.ppermute only.
A program may use at most 256 MiB of HBM per device.

v0:
```python
import jax
import jax.numpy as jnp
from jax import lax
from jax.sharding import PartitionSpec as P

CT = 16
CH = 14
CW = 14
WT = 8
WH = 7
WW = 7
ST = 4
SH = 3
SW = 3
POS = 3136
WIN = 392
NWIN = 8
RB = 2535


def normalize(token_rows, gain, offset):
    row_mean = jnp.mean(token_rows, axis=-1, keepdims=True)
    centered = token_rows - row_mean
    variance = jnp.mean(centered * centered, axis=-1, keepdims=True)
    return centered * lax.rsqrt(variance + 1e-05) * gain + offset


def exact_gelu(values):
    return jax.nn.gelu(values, approximate=False)


def to_windows(field):
    clip_count = field.shape[0]
    features = field.shape[-1]
    grid_cells = field.reshape(clip_count, CT, CH, CW, features)
    grid_cells = jnp.roll(grid_cells, (-ST, -SH, -SW), axis=(1, 2, 3))
    grid_cells = grid_cells.reshape(clip_count, CT // WT, WT, CH // WH, WH, CW // WW, WW, features)
    grid_cells = grid_cells.transpose(0, 1, 3, 5, 2, 4, 6, 7)
    return grid_cells.reshape(clip_count * NWIN, WIN, features)


def from_windows(windows, clip_count):
    features = windows.shape[-1]
    grid_cells = windows.reshape(clip_count, CT // WT, CH // WH, CW // WW, WT, WH, WW, features)
    grid_cells = grid_cells.transpose(0, 1, 4, 2, 5, 3, 6, 7).reshape(
        clip_count, CT, CH, CW, features
    )
    grid_cells = jnp.roll(grid_cells, (ST, SH, SW), axis=(1, 2, 3))
    return grid_cells.reshape(clip_count, CT * CH * CW, features)


def region_part(extent, window, offset):
    places = jnp.arange(extent)
    return jnp.where(places < extent - window, 0, jnp.where(places < extent - offset, 1, 2)).astype(
        jnp.int32
    )


def window_mask():
    regions = (
        region_part(CT, WT, ST)[:, None, None] * 9
        + region_part(CH, WH, SH)[None, :, None] * 3
        + region_part(CW, WW, SW)[None, None, :]
    )
    grid_cells = regions.reshape(CT // WT, WT, CH // WH, WH, CW // WW, WW).transpose(
        0, 2, 4, 1, 3, 5
    )
    grid_cells = grid_cells.reshape(NWIN, WIN)
    return grid_cells[:, :, None] == grid_cells[:, None, :]


def relative_index():
    places = jnp.arange(WIN)
    frames = places // (WH * WW)
    rows_of = places // WW % WH
    column = places % WW
    return (
        (
            (frames[:, None] - frames[None, :] + WT - 1) * (2 * WH - 1)
            + rows_of[:, None]
            - rows_of[None, :]
            + WH
            - 1
        )
        * (2 * WW - 1)
        + column[:, None]
        - column[None, :]
        + WW
        - 1
    )


def window_block(window_count):
    least_windows = -(-512 // WIN)
    for block_try in range(least_windows, window_count + 1):
        return block_try
    return window_count


def masked_scores(query_b, key_b, mask_b, pos_bias, scale):
    scores = (
        jnp.einsum("wqhd,wkhd->whqk", query_b, key_b, preferred_element_type=jnp.float32) * scale
        + pos_bias[None]
    )
    return jnp.where(mask_b[:, None], scores, -1000000000.0)


def per_device(
    tokens,
    grad_out,
    ln1_gain,
    ln1_shift,
    w_qkv,
    qkv_bias,
    rel_table,
    w_proj,
    proj_bias,
    ln2_gain,
    ln2_shift,
    w_in,
    in_bias,
    w_out,
    out_bias,
):
    (
        full_qkv,
        full_in,
        full_proj,
        full_out,
        gain_one,
        shift_one,
        gain_two,
        shift_two,
        proj_shift,
        out_shift,
    ) = (
        lax.all_gather(w_qkv, "grp", axis=0, tiled=True),
        lax.all_gather(w_in, "grp", axis=0, tiled=True),
        lax.all_gather(w_proj, "grp", axis=0, tiled=True),
        lax.all_gather(w_out, "grp", axis=0, tiled=True),
        lax.all_gather(ln1_gain, "grp", axis=0, tiled=True),
        lax.all_gather(ln1_shift, "grp", axis=0, tiled=True),
        lax.all_gather(ln2_gain, "grp", axis=0, tiled=True),
        lax.all_gather(ln2_shift, "grp", axis=0, tiled=True),
        lax.all_gather(proj_bias, "grp", axis=0, tiled=True),
        lax.all_gather(out_bias, "grp", axis=0, tiled=True),
    )
    gain_one = gain_one.astype(jnp.float32)
    shift_one = shift_one.astype(jnp.float32)
    gain_two = gain_two.astype(jnp.float32)
    shift_two = shift_two.astype(jnp.float32)
    proj_shift = proj_shift.astype(jnp.float32)
    out_shift = out_shift.astype(jnp.float32)
    clip_local = tokens.shape[0] // lax.axis_size("grp")
    share_count = tokens.shape[0] // lax.axis_size("tp")
    share_start = lax.axis_index("tp") * share_count

    def own_share(field):
        return lax.dynamic_slice_in_dim(field, share_start, share_count, 0)

    head_local = rel_table.shape[1]
    width_local = w_qkv.shape[2]
    head_size = width_local // head_local
    scale = head_size ** (-0.5)
    window_count = clip_local * NWIN
    block = window_block(window_count)
    blocks = window_count // block
    rel_places = relative_index().reshape(-1)
    table_heads = rel_table.astype(jnp.float32).T
    pos_bias = jnp.take(table_heads, rel_places, axis=1).reshape(head_local, WIN, WIN)
    mask_all = jnp.tile(window_mask(), (clip_local, 1, 1)).reshape(blocks, block, WIN, WIN)

    def split_kinds(window_rows):
        parts = window_rows.reshape(block, WIN, 3, head_local, head_size)
        return (parts[:, :, 0], parts[:, :, 1], parts[:, :, 2])

    inputs = tokens.astype(jnp.float32)
    normed_one, back_one = jax.vjp(normalize, inputs, gain_one, shift_one)
    low_one = normed_one.astype(jnp.bfloat16)
    projected = jnp.einsum("cpd,dkf->cpkf", low_one, full_qkv, preferred_element_type=jnp.float32)
    qkv_shift = jnp.stack([qkv_bias[0], jnp.zeros_like(qkv_bias[0]), qkv_bias[1]]).astype(
        jnp.float32
    )
    qkv_low = (projected + qkv_shift).astype(jnp.bfloat16)
    grouped = lax.all_to_all(qkv_low, "grp", split_axis=0, concat_axis=1, tiled=True)
    windows = to_windows(grouped.reshape(clip_local, POS, 3 * width_local))
    windows = windows.reshape(blocks, block, WIN, 3 * width_local)

    def forward_block(pieces):
        window_rows, mask_b = pieces
        query_b, key_b, value_b = split_kinds(window_rows)
        scores = masked_scores(query_b, key_b, mask_b, pos_bias, scale)
        top = jnp.max(scores, axis=-1, keepdims=True)
        expanded = jnp.exp(scores - top)
        total = jnp.sum(expanded, axis=-1, keepdims=True)
        probs = (expanded / total).astype(jnp.bfloat16)
        attended = jnp.einsum("whqk,wkhd->wqhd", probs, value_b, preferred_element_type=jnp.float32)
        return (
            attended.astype(jnp.bfloat16).reshape(block, WIN, width_local),
            (top + jnp.log(total))[..., 0],
        )

    attended, log_sums = lax.map(forward_block, (windows, mask_all))
    att_pos = from_windows(attended.reshape(window_count, WIN, width_local), clip_local)
    back_pos = lax.all_to_all(att_pos, "grp", split_axis=1, concat_axis=0, tiled=True)
    branch = lax.psum(
        jnp.einsum("cpf,df->cpd", back_pos, full_proj, preferred_element_type=jnp.float32), "tp"
    )
    hidden_one = inputs + branch + proj_shift
    normed_two, back_two = jax.vjp(normalize, hidden_one, gain_two, shift_two)
    low_two = normed_two.astype(jnp.bfloat16)
    inner_act = jnp.einsum(
        "cpd,df->cpf", low_two, full_in, preferred_element_type=jnp.float32
    ) + in_bias.astype(jnp.float32)
    activated, back_gelu = jax.vjp(exact_gelu, inner_act)
    low_act = activated.astype(jnp.bfloat16)
    mlp_part = jnp.einsum("cpf,df->cpd", low_act, full_out, preferred_element_type=jnp.float32)
    mlp_piece = lax.psum_scatter(
        mlp_part.astype(jnp.bfloat16), "tp", scatter_dimension=0, tiled=True
    ).astype(jnp.float32)
    out_piece = (own_share(hidden_one) + mlp_piece + out_shift).astype(jnp.bfloat16)
    output_low = lax.all_gather(out_piece, "tp", axis=0, tiled=True)
    upstream = grad_out.astype(jnp.float32)
    grad_out_shift = jnp.sum(upstream, axis=(0, 1))
    grad_w_out = jnp.einsum("cpd,cpf->df", grad_out, low_act, preferred_element_type=jnp.float32)
    grad_act = jnp.einsum("cpd,df->cpf", grad_out, full_out, preferred_element_type=jnp.float32)
    grad_inner = back_gelu(grad_act)[0].astype(jnp.bfloat16)
    grad_in_bias = jnp.sum(grad_inner, axis=(0, 1), dtype=jnp.float32)
    grad_w_in = jnp.einsum("cpd,cpf->df", low_two, grad_inner, preferred_element_type=jnp.float32)
    norm_term = jnp.einsum("cpf,df->cpd", grad_inner, full_in, preferred_element_type=jnp.float32)
    norm_piece = lax.psum_scatter(norm_term, "tp", scatter_dimension=0, tiled=True)
    unused_two, back_two_piece = jax.vjp(normalize, own_share(hidden_one), gain_two, shift_two)
    hidden_piece, gain_two_piece, shift_two_piece = back_two_piece(norm_piece)
    hidden_piece = hidden_piece + own_share(upstream)
    grad_branch = lax.all_gather(hidden_piece.astype(jnp.bfloat16), "tp", axis=0, tiled=True)
    grad_proj_shift = jnp.sum(grad_branch, axis=(0, 1), dtype=jnp.float32)
    grad_w_proj = jnp.einsum(
        "cpd,cpf->df", grad_branch, back_pos, preferred_element_type=jnp.float32
    )
    grad_att = jnp.einsum(
        "cpd,df->cpf", grad_branch, full_proj, preferred_element_type=jnp.float32
    ).astype(jnp.bfloat16)
    grad_grouped = lax.all_to_all(grad_att, "grp", split_axis=0, concat_axis=1, tiled=True)
    grad_windows = to_windows(grad_grouped).reshape(blocks, block, WIN, width_local)

    def backward_block(pieces):
        window_rows, mask_b, sums_b, grad_rows = pieces
        query_b, key_b, value_b = split_kinds(window_rows)
        grad_b = grad_rows.reshape(block, WIN, head_local, head_size)
        scores = masked_scores(query_b, key_b, mask_b, pos_bias, scale)
        probs = jnp.exp(scores - sums_b[..., None])
        probs_low = probs.astype(jnp.bfloat16)
        grad_probs = jnp.einsum(
            "wqhd,wkhd->whqk", grad_b, value_b, preferred_element_type=jnp.float32
        )
        row_dot = jnp.sum(probs * grad_probs, axis=-1, keepdims=True)
        grad_scores = (probs * (grad_probs - row_dot)).astype(jnp.bfloat16)
        grad_query = (
            jnp.einsum("whqk,wkhd->wqhd", grad_scores, key_b, preferred_element_type=jnp.float32)
            * scale
        )
        grad_key = (
            jnp.einsum("whqk,wqhd->wkhd", grad_scores, query_b, preferred_element_type=jnp.float32)
            * scale
        )
        grad_value = jnp.einsum(
            "whqk,wqhd->wkhd", probs_low, grad_b, preferred_element_type=jnp.float32
        )
        stacked = jnp.concatenate(
            [
                grad_query.astype(jnp.bfloat16).reshape(block, WIN, width_local),
                grad_key.astype(jnp.bfloat16).reshape(block, WIN, width_local),
                grad_value.astype(jnp.bfloat16).reshape(block, WIN, width_local),
            ],
            axis=-1,
        )
        return (stacked, jnp.sum(grad_scores, axis=0, dtype=jnp.float32))

    qkv_grads, bias_parts = lax.map(backward_block, (windows, mask_all, log_sums, grad_windows))
    bias_total = jnp.sum(bias_parts, axis=0).reshape(head_local, WIN * WIN)

    def table_row(head_row):
        return jax.ops.segment_sum(head_row, rel_places, num_segments=RB)

    grad_table = jax.vmap(table_row)(bias_total).T
    grad_pos = from_windows(qkv_grads.reshape(window_count, WIN, 3 * width_local), clip_local)
    grad_pos = grad_pos.reshape(clip_local, POS, 3, width_local)
    grad_qkv = lax.all_to_all(grad_pos, "grp", split_axis=1, concat_axis=0, tiled=True)
    grad_qkv_bias = jnp.stack(
        [
            jnp.sum(grad_qkv[:, :, 0], axis=(0, 1), dtype=jnp.float32),
            jnp.sum(grad_qkv[:, :, 2], axis=(0, 1), dtype=jnp.float32),
        ]
    )
    grad_w_qkv = jnp.einsum("cpd,cpkf->dkf", low_one, grad_qkv, preferred_element_type=jnp.float32)
    first_term = jnp.einsum("cpkf,dkf->cpd", grad_qkv, full_qkv, preferred_element_type=jnp.float32)
    first_piece = lax.psum_scatter(first_term, "tp", scatter_dimension=0, tiled=True)
    unused_one, back_one_piece = jax.vjp(normalize, own_share(inputs), gain_one, shift_one)
    input_piece, gain_one_piece, shift_one_piece = back_one_piece(first_piece)
    collected = (
        lax.all_gather(input_piece + hidden_piece, "tp", axis=0, tiled=True),
        lax.all_gather(gain_one_piece[None], "tp", axis=0, tiled=True),
        lax.all_gather(shift_one_piece[None], "tp", axis=0, tiled=True),
        lax.all_gather(gain_two_piece[None], "tp", axis=0, tiled=True),
        lax.all_gather(shift_two_piece[None], "tp", axis=0, tiled=True),
    )
    grad_tokens = collected[0]
    grad_gain_one = jnp.sum(collected[1], axis=0)
    grad_shift_one = jnp.sum(collected[2], axis=0)
    grad_gain_two = jnp.sum(collected[3], axis=0)
    grad_shift_two = jnp.sum(collected[4], axis=0)
    shares = (
        lax.psum_scatter(grad_w_qkv, "grp", scatter_dimension=0, tiled=True),
        lax.psum_scatter(grad_w_in, "grp", scatter_dimension=0, tiled=True),
        lax.psum_scatter(grad_w_proj, "grp", scatter_dimension=0, tiled=True),
        lax.psum_scatter(grad_w_out, "grp", scatter_dimension=0, tiled=True),
        lax.psum_scatter(grad_gain_one, "grp", scatter_dimension=0, tiled=True),
        lax.psum_scatter(grad_shift_one, "grp", scatter_dimension=0, tiled=True),
        lax.psum_scatter(grad_gain_two, "grp", scatter_dimension=0, tiled=True),
        lax.psum_scatter(grad_shift_two, "grp", scatter_dimension=0, tiled=True),
        lax.psum_scatter(grad_proj_shift, "grp", scatter_dimension=0, tiled=True),
        lax.psum_scatter(grad_out_shift, "grp", scatter_dimension=0, tiled=True),
    )
    head_sums = lax.psum((grad_qkv_bias, grad_in_bias, grad_table), "grp")
    return (
        output_low,
        grad_tokens,
        shares[4],
        shares[5],
        shares[0],
        head_sums[0],
        head_sums[2],
        shares[2],
        shares[8],
        shares[6],
        shares[7],
        shares[1],
        head_sums[1],
        shares[3],
        shares[9],
    )


def solution(mesh):
    placed = (
        P(None, "grp", None),
        P(None, "grp", None),
        P("grp"),
        P("grp"),
        P("grp", None, "tp"),
        P(None, "tp"),
        P(None, "tp"),
        P("grp", "tp"),
        P("grp"),
        P("grp"),
        P("grp"),
        P("grp", "tp"),
        P("tp"),
        P("grp", "tp"),
        P("grp"),
    )
    return jax.shard_map(
        per_device,
        mesh=mesh,
        in_specs=placed,
        out_specs=(
            P(None, "grp", None),
            P(None, "grp", None),
            P("grp"),
            P("grp"),
            P("grp", None, "tp"),
            P(None, "tp"),
            P(None, "tp"),
            P("grp", "tp"),
            P("grp"),
            P("grp"),
            P("grp"),
            P("grp", "tp"),
            P("tp"),
            P("grp", "tp"),
            P("grp"),
        ),
        check_vma=False,
    )
```

profile of v0, /device:TPU:0, one launch (start us, length us, event | category | flops | bytes accessed | tf_op | source)
XLA Modules:
  0.0 2392.9 jit_solution(17466941023475592597)
XLA Ops:
  14.4 23.9 all-reduce.13
  42.4 31.0 %all_gather.53 = bf16[512,3,128]{2,0,1:T(8,128)(2,1)S(1)} all-gather(bf16[64,3,128]{2,0,1:T(8,128)(2,1)S(1)} %copy-done.31), channel_id=1, replica_groups=mesh['grp'=8,'tp'=4] {'grp'}, dimensions={0}, use_global_device_ids=true | all-gather | bytes 442368 | tf_op jit(solution)/shard_map/all_gather | solution.py:137
  86.6 6.4 fusion.48
  93.6 281.4 %gather_fusion = f32[153664,4]{1,0:T(8,128)} fusion(f32[4,2535]{0,1:T(8,128)S(1)} %bitcast.224, s32[154624]{0:T(1024)S(1)} %pad_clamp_fusion), kind=kCustom, calls=%fused_computation | custom fusion | bytes 5531904 | tf_op jit(solution)/shard_map/jit(_take)/gather | solution.py:170
  375.0 78.0 %select_bitcast_fusion = f32[4,153664]{0,1:T(8,128)} fusion(f32[153664,4]{1,0:T(8,128)} %gather_fusion, pred[153664]{0:T(1024)(128)(4,1)S(1)} %compare_and_fusion), kind=kLoop, calls=%fused_computation.41 | loop fusion | flops 614656 | bytes 5070912 | tf_op jit(solution)/shard_map/jit(_take)/select_n | solution.py:170
  453.0 40.2 %copy.129 = f32[4,153664]{1,0:T(4,128)} copy(f32[4,153664]{0,1:T(8,128)} %select_bitcast_fusion) | data formatting | bytes 4917248 | tf_op jit(solution)/shard_map/while | solution.py:203
  515.3 6.3 copy.128
  521.7 95.5 %while.24 = (s32[]{:T(128)}, bf16[4,2,392,128]{3,1,2,0:T(2,128)(2,1)}, f32[4,2,4,392]{3,2,1,0:T(4,128)S(1)}, bf16[4,2,392,384]{2,3,1,0:T(8,128)(2,1)}, pred[4,2,...) while((s32[]{:T(128)}, bf16[4,2,392,128]{3,1,2,0:T(2,128)(2,1)}, ...), condition=%wide.region_5.6_spmd, body=%wide.region_2.5_spmd.sunk | while | flops 175888832 | bytes 37928820 | solution.py:203
  526.0 7.3 add.701
  549.7 7.3 add.701
  573.5 7.3 add.701
  597.3 7.3 add.701
  620.2 17.3 reduce.12
  638.6 6.0 all-to-all-start.1
  644.6 36.8 %all_gather.54 = bf16[512,128]{1,0:T(8,128)(2,1)S(1)} all-gather(bf16[64,128]{1,0:T(8,128)(2,1)S(1)} %copy-done.39), channel_id=1, replica_groups=mesh['grp'=8,'tp'=4] {'grp'}, dimensions={0}, use_global_device_ids=true | all-gather | bytes 147456 | tf_op jit(solution)/shard_map/all_gather | solution.py:139
  688.7 33.6 %all_gather.58 = bf16[512,512]{1,0:T(8,128)(2,1)} all-gather(bf16[64,512]{1,0:T(8,128)(2,1)S(1)} %copy-done.29), channel_id=1, replica_groups=mesh['grp'=8,'tp'=4] {'grp'}, dimensions={0}, use_global_device_ids=true | all-gather | bytes 589824 | tf_op jit(solution)/shard_map/all_gather | solution.py:138
  722.3 33.2 %all_gather.59 = bf16[512,512]{1,0:T(8,128)(2,1)} all-gather(bf16[64,512]{1,0:T(8,128)(2,1)S(1)} %copy-done.30), channel_id=1, replica_groups=mesh['grp'=8,'tp'=4] {'grp'}, dimensions={0}, use_global_device_ids=true | all-gather | bytes 589824 | tf_op jit(solution)/shard_map/all_gather | solution.py:140
  755.5 50.6 %all-reduce.16.cloned.1.call-done = f32[8,392,512]{2,1,0:T(8,128)} async-done(((f32[8,392,512]{2,1,0:T(8,128)}), f32[8,392,512]{2,1,0:T(8,128)}) %all-reduce.16.cloned.1.call-update) | async-done | bytes 6422544 | tf_op jit(solution)/shard_map/psum | solution.py:206
  815.7 15.4 multiply_convert_fusion.1
  842.2 5.5 convolution_convert_fusion
  856.6 45.2 %reduce-scatter.12.cloned.1.call-done = f32[2,392,512]{2,1,0:T(8,128)} async-done(((f32[8,392,512]{2,1,0:T(8,128)}), f32[2,392,512]{2,1,0:T(8,128)}) %reduce-scatter.12.cloned.1.call-update) | async-done | bytes 1605648 | tf_op jit(solution)/shard_map/reduce_scatter | solution.py:231
  904.9 38.0 %reduce-scatter.10.cloned.1.call-done = bf16[2,392,512]{2,1,0:T(8,128)(2,1)} async-done(((bf16[8,392,512]{2,1,0:T(8,128)(2,1)}), bf16[2,392,512]{2,1,0:T(8,128)(2,1)}) %reduce-scatter.10.cloned.1.call-update) | async-done | bytes 802832 | tf_op jit(solution)/shard_map/reduce_scatter | solution.py:218
  950.3 29.1 %all-gather.14.cloned.1.call-done = bf16[8,392,512]{2,1,0:T(8,128)(2,1)} async-done(((bf16[2,392,512]{2,1,0:T(8,128)(2,1)}), bf16[8,392,512]{2,1,0:T(8,128)(2,1)}) %all-gather.14.cloned.1.call-update) | async-done | bytes 3211280 | tf_op jit(solution)/shard_map/all_gather | solution.py:235
  983.2 5.5 all-to-all-start.2
  988.7 20.8 all-to-all-done.2
  1012.8 194.5 %while.25 = (s32[]{:T(128)}, bf16[4,2,392,384]{3,1,2,0:T(2,128)(2,1)}, f32[4,4,392,392]{3,2,1,0:T(8,128)}, bf16[4,2,392,384]{2,3,1,0:T(8,128)(2,1)}, pred[4,2,39...) while((s32[]{:T(128)}, ...), condition=%wide.region_18.19_spmd, body=%wide.region_15.18_spmd.sunk | while | flops 409821888 | bytes 128644888 | solution.py:279
  1021.1 7.3 add.703
  1031.7 5.6 multiply_reduce_fusion.10
  1037.2 10.3 convert_reduce_fusion.8
  1069.7 7.3 add.703
  1080.2 5.6 multiply_reduce_fusion.10
  1085.8 10.3 convert_reduce_fusion.8
  1118.2 7.3 add.703
  1128.8 5.6 multiply_reduce_fusion.10
  1134.4 10.3 convert_reduce_fusion.8
  1166.9 7.3 add.703
  1177.5 5.6 multiply_reduce_fusion.10
  1183.0 10.3 convert_reduce_fusion.8
  1215.3 6.2 reshape_reshape.23
  1221.5 76.5 %all_to_all.42 = bf16[1,3136,3,128]{3,2,0,1:T(4,128)(2,1)S(1)} all-to-all(bf16[1,3136,3,128]{3,2,0,1:T(4,128)(2,1)S(1)} %bitcast.240), channel_id=1, replica_groups=mesh['grp'=8,'tp'=4] {'grp'}, dimensions={1} | all-to-all | bytes 4816896 | tf_op jit(solution)/shard_map/all_to_all | solution.py:288
  1310.3 51.0 %reduce-scatter.14.cloned.1.call-done = f32[2,392,512]{2,1,0:T(8,128)} async-done(((f32[8,392,512]{2,1,0:T(8,128)}), f32[2,392,512]{2,1,0:T(8,128)}) %reduce-scatter.14.cloned.1.call-update) | async-done | bytes 1605648 | tf_op jit(solution)/shard_map/reduce_scatter | solution.py:297
  1370.1 8.2 convolution_bitcast_fusion.2
  1378.6 5.9 convolution_bitcast_fusion.1
  1391.2 5.5 fusion.35
  1411.0 8.5 reduce_sum.311
  1419.5 46.8 %copy.155 = f32[4,392,392]{0,2,1:T(8,128)} copy(f32[4,392,392]{2,1,0:T(8,128)} %reduce_sum.311) | data formatting | bytes 4917248 | tf_op jit(solution)/shard_map/reshape | solution.py:280
  1466.3 820.0 %scatter_custom_fusion = f32[4,2535]{0,1:T(8,128)} fusion(s32[153664]{0:T(1024)} %copy-done.20, f32[153664,4]{1,0:T(8,128)} %bitcast.55, f32[]{:T(128)} %constant.90.clone.1), kind=kCustom, calls=%fused_computation.139 | custom fusion | flops 614656 | bytes 41072 | tf_op jit(solution)/shard_map/vmap()/scatter-add | solution.py:283
  2297.1 76.8 %all-reduce.12 = (f32[512]{0:T(512)S(1)}, f32[512]{0:T(512)S(1)}, f32[2,128]{1,0:T(2,128)}, f32[2535,4]{1,0:T(8,128)S(1)}, f32[512]{0:T(512)S(1)}, /*index=5*/f3...) all-reduce(f32[512]{0:T(512)S(1)} %reduce_sum.306, ...), channel_id=9, replica_groups=mesh['grp'=8,'tp'=4] {'grp'}, use_global_device_ids=true, to_apply=%region_26.27.clone | all-reduce | flops 13980 | bytes 111840
  (424 shorter events, 343.7 us)
Async XLA Ops:
  7.2 33.7 %copy-start.6 = (bf16[8,392,512]{2,1,0:T(8,128)(2,1)S(1)}, bf16[8,392,512]{2,1,0:T(8,128)(2,1)}, u32[]{:S(2)}) copy-start(bf16[8,392,512]{2,1,0:T(8,128)(2,1)} %param.19) | copy-start | bytes 9633796
  7.2 35.2 %copy-start.51 = (bf16[2,128]{1,0:T(2,128)(2,1)S(1)}, bf16[2,128]{1,0:T(2,128)(2,1)}, u32[]{:S(2)}) copy-start(bf16[2,128]{1,0:T(2,128)(2,1)} %param.24) | copy-start | bytes 1540
  7.2 35.2 %copy-start.31 = (bf16[64,3,128]{2,0,1:T(8,128)(2,1)S(1)}, bf16[64,3,128]{2,0,1:T(8,128)(2,1)}, u32[]{:S(2)}) copy-start(bf16[64,3,128]{2,0,1:T(8,128)(2,1)} %param.23) | copy-start | bytes 147460
  38.3 35.3 %copy-start.34 = (f32[512]{0:T(512)}, f32[512]{0:T(512)S(1)}, u32[]{:S(2)}) copy-start(f32[512]{0:T(512)S(1)} %convert_element_type.116) | copy-start | bytes 6148
  38.3 35.3 %copy-start.47 = (f32[512]{0:T(512)}, f32[512]{0:T(512)S(1)}, u32[]{:S(2)}) copy-start(f32[512]{0:T(512)S(1)} %convert_element_type.117) | copy-start | bytes 6148
  40.9 32.7 %copy-start.25 = (f32[8,392]{1,0:T(8,128)}, f32[8,392]{1,0:T(8,128)S(1)}, u32[]{:S(2)}) copy-start(f32[8,392]{1,0:T(8,128)S(1)} %broadcast_multiply_fusion.1) | copy-start | bytes 37636
  42.4 31.2 %copy-start.40 = (f32[8,392]{1,0:T(8,128)}, f32[8,392]{1,0:T(8,128)S(1)}, u32[]{:S(2)}) copy-start(f32[8,392]{1,0:T(8,128)S(1)} %add_rsqrt_fusion.1) | copy-start | bytes 37636
  77.7 418.1 %all-to-all-start = ((bf16[8,392,3,128]{3,1,2,0:T(8,128)(2,1)}), bf16[8,392,3,128]{3,1,2,0:T(8,128)(2,1)}, u32[]{:S(2)}, u32[]{:S(2)}) async-start(bf16[8,392,3,128]{3,1,2,0:T(8,128)(2,1)} %add_convert_fusion.3), calls=%async_computation | async-start | bytes 4816896 | tf_op jit(solution)/shard_map/all_to_all | solution.py:185
  82.3 10.8 copy-start.36
  83.5 10.1 copy-start.20
  618.9 25.6 %copy-start.39 = (bf16[64,128]{1,0:T(8,128)(2,1)S(1)}, bf16[64,128]{1,0:T(8,128)(2,1)}, u32[]{:S(2)}) copy-start(bf16[64,128]{1,0:T(8,128)(2,1)} %param.26) | copy-start | bytes 49156
  638.6 42.9 %all-to-all-start.1 = ((bf16[8,2,25088]{2,1,0:T(2,128)(2,1)}), bf16[8,2,25088]{2,1,0:T(2,128)(2,1)S(1)}, u32[]{:S(2)}, u32[]{:S(2)}) async-start(bf16[8,2,25088]{2,1,0:T(2,128)(2,1)} %reshape.655), calls=%async_computation.1 | async-start | bytes 1605632 | tf_op jit(solution)/shard_map/all_to_all | solution.py:205
  644.5 161.6 %all-reduce.16.cloned.1.call-start = ((), (), s32[]{:S(2)}) async-start(), calls=%async_computation.11 | async-start | bytes 12845056 | tf_op jit(solution)/shard_map/psum | solution.py:206
  687.0 35.4 %copy-start.30 = (bf16[64,512]{1,0:T(8,128)(2,1)S(1)}, bf16[64,512]{1,0:T(8,128)(2,1)}, u32[]{:S(2)}) copy-start(bf16[64,512]{1,0:T(8,128)(2,1)} %param.32) | copy-start | bytes 196612
  687.0 119.2 %copy-start.7 = (bf16[8,392,512]{2,1,0:T(8,128)(2,1)S(1)}, bf16[8,392,512]{2,1,0:T(8,128)(2,1)}, u32[]{:S(2)}) copy-start(bf16[8,392,512]{2,1,0:T(8,128)(2,1)} %param.19) | copy-start | bytes 9633796
  687.0 214.7 %reduce-scatter.12.cloned.1.call-start = ((), (), s32[]{:S(2)}) async-start(), calls=%async_computation.14 | async-start | bytes 8028160 | tf_op jit(solution)/shard_map/reduce_scatter | solution.py:231
  687.6 255.3 %copy-start.37 = (f32[512]{0:T(512)}, f32[512]{0:T(512)S(1)}, u32[]{:S(2)}) copy-start(f32[512]{0:T(512)S(1)} %convert_element_type.122) | copy-start | bytes 6148
  687.7 123.8 %copy-start.49 = (f32[512]{0:T(512)}, f32[512]{0:T(512)S(1)}, u32[]{:S(2)}) copy-start(f32[512]{0:T(512)S(1)} %convert_element_type.123) | copy-start | bytes 6148
  815.7 15.4 copy-start.9
  815.7 15.4 copy-start.24
  842.2 100.7 %reduce-scatter.10.cloned.1.call-start = ((), (), s32[]{:S(2)}) async-start(), calls=%async_computation.12 | async-start | bytes 4014080 | tf_op jit(solution)/shard_map/reduce_scatter | solution.py:218
  847.8 131.5 %all-gather.14.cloned.1.call-start = ((), (), s32[]{:S(2)}) async-start(), calls=%async_computation.15 | async-start | bytes 4014080 | tf_op jit(solution)/shard_map/all_gather | solution.py:235
  946.6 36.6 %copy-start.32 = (f32[2,392]{1,0:T(2,128)}, f32[2,392]{1,0:T(2,128)S(1)}, u32[]{:S(2)}) copy-start(f32[2,392]{1,0:T(2,128)S(1)} %negate_multiply_fusion.2) | copy-start | bytes 9412
  983.2 26.4 %all-to-all-start.2 = ((bf16[8,392,128]{2,1,0:T(8,128)(2,1)}), bf16[8,392,128]{2,1,0:T(8,128)(2,1)S(1)}, u32[]{:S(2)}, u32[]{:S(2)}) async-start(bf16[8,392,128]{2,1,0:T(8,128)(2,1)} %convolution_convert_fusion.1), calls=%async_computation.4 | async-start | bytes 1605632 | tf_op jit(solution)/shard_map/all_to_all | solution.py:243
  988.7 372.6 %reduce-scatter.14.cloned.1.call-start = ((), (), s32[]{:S(2)}) async-start(), calls=%async_computation.16 | async-start | bytes 8028160 | tf_op jit(solution)/shard_map/reduce_scatter | solution.py:297
  1014.0 7.1 copy-start.2
  1037.2 10.3 copy-start
  1047.5 10.6 slice-start
  1085.8 10.3 copy-start
  1096.1 10.6 slice-start
  1134.4 10.3 copy-start
  1144.7 10.7 slice-start
  1183.0 10.3 copy-start
  1193.3 10.6 slice-start
  1221.5 78.3 %copy-start.23 = (bf16[512,3,128]{2,0,1:T(8,128)(2,1)S(1)}, bf16[512,3,128]{2,0,1:T(8,128)(2,1)}, u32[]{:S(2)}) copy-start(bf16[512,3,128]{2,0,1:T(8,128)(2,1)} %copy-done.22) | copy-start | bytes 1179652
  1304.4 106.1 %all-gather.12.cloned.1.call-start = ((), (), s32[]{:S(2)}) async-start(), calls=%async_computation.13 | async-start | bytes 4014080 | tf_op jit(solution)/shard_map/all_gather | solution.py:222
  1305.0 56.3 %copy-start.35 = (f32[512]{0:T(512)S(1)}, f32[512]{0:T(512)}, u32[]{:S(2)}) copy-start(f32[512]{0:T(512)} %copy-done.34) | copy-start | bytes 6148
  1305.0 1073.4 %all-gather.16.cloned.1.call-start = ((), (), s32[]{:S(2)}) async-start(), calls=%async_computation.17 | async-start | bytes 8028160 | tf_op jit(solution)/shard_map/all_gather | solution.py:301
  1310.1 56.6 %copy-start.33 = (f32[2,392]{1,0:T(2,128)S(1)}, f32[2,392]{1,0:T(2,128)}, u32[]{:S(2)}) copy-start(f32[2,392]{1,0:T(2,128)} %copy-done.32) | copy-start | bytes 9412
  1370.0 1008.4 %reduce-scatter.20.cloned.1.call-start = ((), (), s32[]{:S(2)}) async-start(), calls=%async_computation.20 | async-start | bytes 1179648 | tf_op jit(solution)/shard_map/reduce_scatter | solution.py:314
  1378.3 1000.1 %reduce-scatter.22.cloned.1.call-start = ((), (), s32[]{:S(2)}) async-start(), calls=%async_computation.21 | async-start | bytes 1179648
  1387.1 991.3 %reduce-scatter.18.cloned.1.call-start = ((), (), s32[]{:S(2)}) async-start(), calls=%async_computation.19 | async-start | bytes 294912 | tf_op jit(solution)/shard_map/reduce_scatter | solution.py:315
  1391.1 9.0 copy-start.45
  1391.1 14.2 copy-start.44
  1391.1 987.4 %reduce-scatter.16.cloned.1.call-start = ((), (), s32[]{:S(2)}) async-start(), calls=%async_computation.18 | async-start | bytes 884736 | tf_op jit(solution)/shard_map/reduce_scatter | solution.py:313
  1396.7 13.8 copy-start.16
  1419.5 866.8 %copy-start.12 = (bf16[1,3136,3,128]{3,1,2,0:T(8,128)(2,1)S(1)}, bf16[1,3136,3,128]{3,1,2,0:T(8,128)(2,1)}, u32[]{:S(2)}) copy-start(bf16[1,3136,3,128]{3,1,2,0:T(8,128)(2,1)} %copy-done.11) | copy-start | bytes 7225348
  1419.5 877.6 %copy-start.46 = (f32[512]{0:T(512)S(1)}, f32[512]{0:T(512)}, u32[]{:S(2)}) copy-start(f32[512]{0:T(512)} %get-tuple-element.288) | copy-start | bytes 6148
  (45 other events, 175.4 us)
Sparse Core Ops, SparseCore 0:
  687.1 118.9 all-reduce.15
  842.3 59.3 reduce-scatter.11
  904.5 38.3 reduce-scatter.9
  950.4 28.8 all-gather.13
  1304.5 56.7 reduce-scatter.13
  1362.8 28.9 all-gather.11
  1393.9 47.1 all-gather.15
  1445.5 63.5 reduce-scatter.19
  1513.1 62.4 reduce-scatter.21
  1579.7 60.2 reduce-scatter.17
  1644.3 62.2 reduce-scatter.15
where the time goes:
time: 2400 us; the launch traced here: 2390 us
  other arithmetic  1050 us (44%)
  local copies, waits for them, and re-layouts  610 us (25%)
  blocking collectives  332 us (14%)
  waiting for transfers between devices  235 us (10%)
  matrix products  132 us (6%)
    scatter-add x1, other arithmetic, table_row(): return jax.ops.segment_sum(head_row, rel_places, num_segments=RB)  820 us
    gather x1, local copies, waits for them, and re-layouts, per_device(): jnp.take(table_heads, rel_places, axis=1).reshape(head_local, WIN, WIN)  281 us
    unnamed x2, blocking collectives  101 us
    add x16, local copies, waits for them, and re-layouts, masked_scores(): jnp.einsum('wqhd,wkhd->whqk', query_b, key_b, preferred_element_type=jnp....  84.6 us
    select_n x2, other arithmetic, per_device(): jnp.take(table_heads, rel_places, axis=1).reshape(head_local, WIN, WIN)  84.4 us
    all_to_all x1, blocking collectives, per_device(): lax.all_to_all(grad_pos, 'grp', split_axis=1, concat_axis=0, tiled=True)  76.5 us
    reduce_scatter x1, waiting for transfers between devices, per_device(): lax.psum_scatter(first_term, 'tp', scatter_dimension=0, tiled=True)  51 us
    psum x1, waiting for transfers between devices, per_device(): lax.psum(jnp.einsum('cpf,df->cpd', back_pos, full_proj, preferred_element...  50.6 us
  transfers between devices with their start and end apart: 14, of which 6 were waited for; matrix products, arithmetic and copies ran while one was open for 56% of the time, Pallas kernels for 0%

commit v1 on v0

v1 whole, which is shorter than its diff:
```python
import functools

import jax
import jax.numpy as jnp
from jax import lax
from jax.experimental import pallas as pl
from jax.experimental.pallas import tpu as pltpu
from jax.sharding import PartitionSpec as P

CT, CH, CW = 16, 14, 14
WT, WH, WW = 8, 7, 7
ST, SH, SW = 4, 3, 3
FRAME = CH * CW
SIDE = WH * WW
WIN = WT * SIDE
PAIR = 2
PADDED = -(-WIN // 16) * 16
ROWS = PAIR * PADDED
HEAD = 32
GROUP = 128
HEADS_IN = GROUP // HEAD
SPAN_T, SPAN_H, SPAN_W = 2 * WT - 1, 2 * WH - 1, 2 * WW - 1
PLANE = SPAN_H * SPAN_W
TABLE = SPAN_T * PLANE
TABLE_PAD = -(-TABLE // 128) * 128
DIAG = SPAN_T * SIDE
DIAG_PAD = -(-DIAG // 128) * 128
SIDE_PAD = -(-SIDE // 8) * 8
CORNER = PLANE // 2
LOG2E = 1.4426950408889634
SCALE = HEAD ** (-0.5)
FAR = -(2.0**100)
f32 = jnp.float32
bf16 = jnp.bfloat16
PARAMS = functools.partial(pltpu.CompilerParams, vmem_limit_bytes=56 * 1024 * 1024)


def cost(micros):
    return pl.CostEstimate(flops=int(micros * 1.1e9), bytes_accessed=1 << 20, transcendentals=0)


def dot(a, b):
    return lax.dot_general(a, b, (((1,), (0,)), ((), ())), preferred_element_type=f32)


def dot_t(a, b):
    return lax.dot_general(a, b, (((1,), (1,)), ((), ())), preferred_element_type=f32)


def moments(rows):
    centered = rows - jnp.mean(rows, axis=-1, keepdims=True)
    inverse = lax.rsqrt(jnp.mean(centered * centered, axis=-1, keepdims=True) + 1e-05)
    return centered * inverse, inverse


def norm_back(grad, unit, inverse, gain):
    scaled = grad * gain
    shared = jnp.mean(scaled, axis=-1, keepdims=True)
    along = jnp.mean(scaled * unit, axis=-1, keepdims=True)
    return inverse * (scaled - shared - unit * along)


def bias_kernel(table_ref, pick_ref, bias_ref, sheared, spread):
    heads = table_ref.shape[0]
    row_of = lax.broadcasted_iota(jnp.int32, (8, TABLE_PAD), 0)
    for head in range(heads):
        flat = jnp.broadcast_to(table_ref[head], (8, TABLE_PAD))
        stairs = flat
        for step in range(1, WW):
            stairs = jnp.where(row_of == step, pltpu.roll(flat, step, 1), stairs)
        for row in range(WH):
            shift = (row * SPAN_W - CORNER) % TABLE_PAD
            sheared[head, pl.ds(row * WW, 8), :] = pltpu.roll(stairs, shift, 1)
    everything = sheared[...].reshape(heads * SIDE_PAD, TABLE_PAD).astype(bf16)
    spread[...] = dot(everything, pick_ref[...]).reshape(heads, SIDE_PAD, DIAG_PAD) * LOG2E
    for head in range(heads):
        block = spread[head]
        for frame in range(WT):
            shift = -(WT - 1 - frame) * SIDE % DIAG_PAD
            moved = pltpu.roll(block, shift, 1) if shift else block
            bias_ref[head, pl.ds(frame * SIDE, SIDE_PAD), :] = moved[:, :PADDED]


def table_kernel(sums_ref, pick_ref, grad_ref, spread, sheared):
    heads = sums_ref.shape[0]
    row_of = lax.broadcasted_iota(jnp.int32, (SIDE_PAD, DIAG_PAD), 0)
    lane_of = lax.broadcasted_iota(jnp.int32, (SIDE_PAD, DIAG_PAD), 1)
    blank = jnp.zeros((SIDE_PAD, DIAG_PAD - PADDED), f32)
    for head in range(heads):
        total = jnp.zeros((SIDE_PAD, DIAG_PAD), f32)
        for frame in range(WT):
            piece = sums_ref[head, pl.ds(frame * SIDE, SIDE_PAD), :]
            piece = jnp.concatenate([piece, blank], axis=1)
            piece = jnp.where(lane_of < WIN, piece, 0.0)
            shift = (WT - 1 - frame) * SIDE
            total = total + (pltpu.roll(piece, shift, 1) if shift else piece)
        spread[head] = jnp.where(row_of < SIDE, total, 0.0)
    everything = spread[...].reshape(heads * SIDE_PAD, DIAG_PAD)
    high = everything.astype(bf16)
    low = (everything - high.astype(f32)).astype(bf16)
    grads = dot_t(high, pick_ref[...]) + dot_t(low, pick_ref[...])
    sheared[...] = grads.reshape(heads, SIDE_PAD, TABLE_PAD)
    row_in = lax.broadcasted_iota(jnp.int32, (8, TABLE_PAD), 0)
    for head in range(heads):
        stairs = jnp.zeros((8, TABLE_PAD), f32)
        for row in range(WH):
            shift = (CORNER - row * SPAN_W) % TABLE_PAD
            stairs = stairs + pltpu.roll(sheared[head, pl.ds(row * WW, 8), :], shift, 1)
        flat = jnp.where(row_in == 0, stairs, 0.0)
        for step in range(1, WW):
            moved = pltpu.roll(stairs, TABLE_PAD - step, 1)
            flat = flat + jnp.where(row_in == step, moved, 0.0)
        grad_ref[head] = jnp.sum(flat, axis=0, keepdims=True)


def attention_kernel(first, *refs):
    if first:
        x_ref, gain_ref, shift_ref, w_ref, wb_ref, bias_ref, qf_ref, kf_ref = refs[:8]
        a1_ref, a1_t_ref, qkv_ref, o_ref, lse_ref = refs[8:]
        unit, _ = moments(x_ref[...].astype(f32))
        low = unit * gain_ref[...] + shift_ref[...]
        a1_ref[...] = low.astype(bf16)
        a1_t_ref[...] = low.T.astype(bf16)
    else:
        a1_ref, w_ref, wb_ref, bias_ref, qf_ref, kf_ref = refs[:6]
        qkv_ref, o_ref, lse_ref = refs[6:]
    qkv_ref[...] = (dot(a1_ref[...], w_ref[...]) + wb_ref[...]).astype(bf16)
    lane = lax.broadcasted_iota(jnp.int32, (PADDED, GROUP), 1) // HEAD
    for window in range(PAIR):
        rows = slice(window * PADDED, (window + 1) * PADDED)
        query = qkv_ref[rows, 0:GROUP]
        key = qkv_ref[rows, GROUP : 2 * GROUP]
        value = qkv_ref[rows, 2 * GROUP : 3 * GROUP]
        query = jnp.concatenate([query, qf_ref[window]], axis=1)
        value_t = value.astype(f32).T.astype(bf16)
        parts = []
        for head in range(HEADS_IN):
            own = jnp.where(lane == head, key, jnp.zeros_like(key))
            own = jnp.concatenate([own, kf_ref[window]], axis=1)
            logits = dot_t(own, query) * (SCALE * LOG2E) + bias_ref[head]
            top = jnp.max(logits, axis=0, keepdims=True)
            probs = jnp.exp2(logits - top)
            total = jnp.sum(probs, axis=0, keepdims=True)
            lse_ref[pl.ds(window * HEADS_IN + head, 1), :] = top + jnp.log2(total)
            mixed = dot(value_t[head * HEAD : (head + 1) * HEAD], probs.astype(bf16))
            parts.append(mixed / total)
        o_ref[rows, :] = jnp.concatenate(parts, axis=0).T.astype(bf16)


def mlp_kernel(
    x_ref, o0_ref, o1_ref, o2_ref, o3_ref, g_ref, home_in, away_in, home_out, away_out,
    pb_ref, gain_ref, shift_ref, ib_ref, ob_ref,
    out_ref, dh_ref, dow_ref, gwi_keep, gwi_send, gwo_keep, gwo_send, gwp_keep, gwp_send,
    gib_ref, vec_ref,
    hidden, a2, a2_t, g_t, unit_s, inv_s, acc_out, acc_in, o_all, wp, wi, wo,
):
    step = pl.program_id(0)
    width = x_ref.shape[1]
    units = home_out.shape[2]

    @pl.when(step == 0)
    def _():
        for i, (o_ref, w_ref, j) in enumerate(
            [(o0_ref, home_in, 0), (o1_ref, away_in, 0), (o2_ref, home_in, 1), (o3_ref, away_in, 1)]
        ):
            o_all[:, i * GROUP : (i + 1) * GROUP] = o_ref[...]
            wp[:, i * GROUP : (i + 1) * GROUP] = w_ref[j, :, units : units + GROUP]
        branch = dot_t(o_all[...], wp[...])
        hidden[...] = x_ref[...].astype(f32) + branch + pb_ref[...]
        unit, inverse = moments(hidden[...])
        unit_s[...] = unit
        inv_s[...] = inverse
        low = unit * gain_ref[...] + shift_ref[...]
        a2[...] = low.astype(bf16)
        a2_t[...] = low.T.astype(bf16)
        g_t[...] = g_ref[...].astype(f32).T.astype(bf16)
        acc_out[...] = jnp.zeros_like(acc_out)
        acc_in[...] = jnp.zeros_like(acc_in)

    for place, (in_ref, out_w, j) in enumerate(
        [(away_in, away_out, 0), (away_in, away_out, 1), (home_in, home_out, 0), (home_in, home_out, 1)]
    ):

        @pl.when(step == place)
        def _():
            wi[...] = in_ref[j, :, 0:units]
            wo[...] = out_w[j]

    u = dot(a2[...], wi[...]) + ib_ref[0]
    half = 0.5 * (1.0 + lax.erf(u * (0.5**0.5)))
    act = (u * half).astype(bf16)
    acc_out[...] += dot_t(act, wo[...])
    back = dot(g_ref[...], wo[...])
    slope = half + u * jnp.exp(-0.5 * u * u) * 0.3989422804014327
    du_low = (back * slope).astype(bf16)
    acc_in[...] += dot_t(du_low, wi[...])
    grad_out_w = dot(g_t[...], act)
    grad_in_w = dot(a2_t[...], du_low)
    gib_ref[0] = jnp.sum(du_low.astype(f32), axis=0, keepdims=True)

    @pl.when(step < 2)
    def _():
        gwo_send[0] = grad_out_w.astype(bf16)
        gwi_send[0] = grad_in_w.astype(bf16)

    @pl.when(step >= 2)
    def _():
        gwo_keep[0] = grad_out_w
        gwi_keep[0] = grad_in_w

    @pl.when(step == pl.num_programs(0) - 1)
    def _():
        out_ref[...] = (hidden[...] + acc_out[...] + ob_ref[...]).astype(bf16)
        upstream = g_ref[...].astype(f32)
        grad = acc_in[...]
        unit = unit_s[...]
        dh = upstream + norm_back(grad, unit, inv_s[...], gain_ref[...])
        dh_ref[...] = dh
        dz = dh.astype(bf16)
        dow_ref[...] = dot(dz, wp[...]).astype(bf16)
        grad_wp = dot(dz.astype(f32).T.astype(bf16), o_all[...])
        for i in range(2):
            gwp_keep[i] = grad_wp[:, 2 * i * GROUP : (2 * i + 1) * GROUP]
            gwp_send[i] = grad_wp[:, (2 * i + 1) * GROUP : (2 * i + 2) * GROUP].astype(bf16)
        vec_ref[...] = jnp.concatenate(
            [
                jnp.sum(grad * unit, axis=0, keepdims=True),
                jnp.sum(grad, axis=0, keepdims=True),
                jnp.sum(dz.astype(f32), axis=0, keepdims=True),
                jnp.sum(upstream, axis=0, keepdims=True),
            ],
            axis=0,
        )


def attention_back_kernel(
    first, last, a1_t_ref, w_ref, qkv_ref, dow_ref, lse_ref, bias_ref, qf_ref, kf_ref, *refs
):
    if last:
        acc_ref, x_ref, gain_ref, dh_ref, gx_ref, vec_ref, gw_ref, gb_ref, sums_ref, dqkv = refs
    elif first:
        out_ref, gw_ref, gb_ref, sums_ref, dqkv = refs
    else:
        acc_ref, out_ref, gw_ref, gb_ref, sums_ref, dqkv = refs
    lane = lax.broadcasted_iota(jnp.int32, (PADDED, GROUP), 1) // HEAD
    for window in range(PAIR):
        rows = slice(window * PADDED, (window + 1) * PADDED)
        query = qkv_ref[rows, 0:GROUP]
        key = qkv_ref[rows, GROUP : 2 * GROUP]
        value = qkv_ref[rows, 2 * GROUP : 3 * GROUP]
        dow = dow_ref[rows, :]
        query_f = jnp.concatenate([query, qf_ref[window]], axis=1)
        key_t = key.astype(f32).T.astype(bf16)
        none = jnp.zeros((PADDED, GROUP), f32)
        dk, dv, dq_t = none, none, []
        for head in range(HEADS_IN):
            mine = lane == head
            own = jnp.where(mine, key, jnp.zeros_like(key))
            own = jnp.concatenate([own, kf_ref[window]], axis=1)
            logits = dot_t(own, query_f) * (SCALE * LOG2E) + bias_ref[head]
            probs = jnp.exp2(logits - lse_ref[pl.ds(window * HEADS_IN + head, 1), :])
            dp = dot_t(jnp.where(mine, value, jnp.zeros_like(value)), dow)
            dots = jnp.sum(probs * dp, axis=0, keepdims=True)
            ds = (probs * (dp - dots)).astype(bf16)
            if window == 0:
                sums_ref[head] = ds.astype(f32)
            else:
                sums_ref[head] += ds.astype(f32)
            dv = jnp.where(mine, dot(probs.astype(bf16), dow), dv)
            dk = jnp.where(mine, dot(ds, query), dk)
            dq_t.append(dot(key_t[head * HEAD : (head + 1) * HEAD], ds))
        dq = jnp.concatenate(dq_t, axis=0).T
        dqkv[rows, 0:GROUP] = (dq * SCALE).astype(bf16)
        dqkv[rows, GROUP : 2 * GROUP] = (dk * SCALE).astype(bf16)
        dqkv[rows, 2 * GROUP : 3 * GROUP] = dv.astype(bf16)
    grad = dot_t(dqkv[...], w_ref[...])
    if not first:
        grad = grad + acc_ref[...]
    gw_ref[...] = dot(a1_t_ref[...], dqkv[...]).astype(gw_ref.dtype)
    gb_ref[...] = jnp.sum(dqkv[...].astype(f32), axis=0, keepdims=True)
    if last:
        unit, inverse = moments(x_ref[...].astype(f32))
        gx_ref[...] = (dh_ref[...] + norm_back(grad, unit, inverse, gain_ref[...])).astype(bf16)
        vec_ref[...] = jnp.concatenate(
            [jnp.sum(grad * unit, axis=0, keepdims=True), jnp.sum(grad, axis=0, keepdims=True)],
            axis=0,
        )
    else:
        out_ref[...] = grad


def whole(shape):
    return pl.BlockSpec(shape, lambda *i: (0,) * len(shape))


def shaped(shape, kind=f32):
    return jax.ShapeDtypeStruct(shape, kind)


def pick_matrix():
    place = lax.iota(jnp.int32, TABLE_PAD)
    row, column = place % PLANE // SPAN_W, place % PLANE % SPAN_W
    target = place // PLANE * SIDE + row * WW + column
    good = (place < TABLE) & (row < WH) & (column < WW)
    target = lax.optimization_barrier(jnp.where(good, target, -1))
    lane = lax.broadcasted_iota(jnp.int32, (TABLE_PAD, DIAG_PAD), 1)
    return (lane == target[:, None]).astype(bf16)


def region_features(late, low):
    cell = lax.broadcasted_iota(jnp.int32, (PAIR, PADDED, GROUP), 1)
    lane = lax.broadcasted_iota(jnp.int32, (PAIR, PADDED, GROUP), 2)
    right = lax.broadcasted_iota(jnp.int32, (PAIR, PADDED, GROUP), 0)
    code = (
        (late * (cell // SIDE >= WT - ST)) * 4
        + (low * (cell // WW % WH >= WH - SH)) * 2
        + right * (cell % WW >= WW - SW)
    )
    real = cell < WIN
    ours = (real & (lane == code)) | (lane == 8)
    theirs = jnp.where(real, (lane < 8) & (lane != code), lane == 8)
    return ours.astype(bf16), jnp.where(theirs, FAR, 0.0).astype(bf16)


class Windows:
    def __init__(self, clips, local, groups, shares):
        self.share = clips // shares
        self.local = local
        self.half = groups // 2
        first = ST * FRAME // local
        order = [(first + i) % groups for i in range(groups)]
        self.groups = [order[: self.half], order[self.half :]]
        self.frames = local // FRAME if local % FRAME == 0 else 0
        slot = (lax.axis_index("grp") - first) % groups
        self.late = slot // self.half
        self.low = slot % 2

    def exchange(self, rows):
        return lax.all_to_all(
            rows, "grp", split_axis=0, concat_axis=0, tiled=True, axis_index_groups=self.groups
        )

    def gather(self, field):
        width = field.shape[-1]
        if self.frames:
            cells = field.reshape(self.share, self.frames, CH, CW, width)
            cells = jnp.roll(cells, (-SH, -SW), axis=(2, 3))
            cells = cells.reshape(self.share, self.frames, 2, WH, 2, WW, width)
            cells = cells.transpose(0, 2, 4, 1, 3, 5, 6)
            cells = self.exchange(cells.reshape(self.half, 2, self.frames * SIDE, width))
            cells = cells.transpose(1, 0, 2, 3).reshape(PAIR, WIN, width)
        else:
            cells = self.exchange(jnp.repeat(field, 2, axis=0))
            cells = cells.reshape(WT, CH, CW, width)
            cells = jnp.roll(cells, (-SH, -SW), axis=(1, 2))
            cells = lax.dynamic_slice_in_dim(cells, self.low * WH, WH, 1)
            cells = cells.reshape(WT, WH, 2, WW, width).transpose(2, 0, 1, 3, 4)
            cells = cells.reshape(PAIR, WIN, width)
        cells = jnp.pad(cells, ((0, 0), (0, PADDED - WIN), (0, 0)))
        return cells.reshape(ROWS, width)

    def scatter(self, rows):
        width = rows.shape[-1]
        cells = rows.reshape(PAIR, PADDED, width)[:, :WIN]
        if self.frames:
            cells = cells.reshape(PAIR, self.half, self.frames * SIDE, width)
            cells = self.exchange(cells.transpose(1, 0, 2, 3))
            cells = cells.reshape(self.share, 2, 2, self.frames, WH, WW, width)
            cells = cells.transpose(0, 3, 1, 4, 2, 5, 6)
            cells = cells.reshape(self.share, self.frames, CH, CW, width)
            cells = jnp.roll(cells, (SH, SW), axis=(2, 3))
        else:
            cells = cells.reshape(2, WT, WH, WW, width).transpose(1, 2, 0, 3, 4)
            cells = cells.reshape(WT, WH, CW, width)
            blank = jnp.zeros((WT, CH, CW, width), cells.dtype)
            cells = lax.dynamic_update_slice_in_dim(blank, cells, self.low * WH, 1)
            cells = jnp.roll(cells, (SH, SW), axis=(1, 2))
            cells = self.exchange(cells.reshape(self.half, self.local, width))
            cells = cells.reshape(self.share, 2, self.local, width)
            cells = cells[:, 0] + cells[:, 1]
        return gather_over(cells.reshape(self.share, self.local, width), "tp", 0)


def swap(field, axis, bit):
    size = lax.axis_size(axis)
    return lax.ppermute(field, axis, [(i, i ^ bit) for i in range(size)])


def bits_of(axis):
    size = lax.axis_size(axis)
    return [1 << i for i in reversed(range(size.bit_length() - 1))]


def flag_of(axis, bit):
    return lax.axis_index(axis) // bit % 2


def gather_over(part, axis, lead):
    bits = bits_of(axis)
    shape = part.shape
    part = part.reshape(shape[:lead] + (1,) * len(bits) + shape[lead:])
    for place, bit in enumerate(bits):
        other = swap(part, axis, bit)
        second = flag_of(axis, bit) == 1
        part = jnp.concatenate(
            [jnp.where(second, other, part), jnp.where(second, part, other)], axis=lead + place
        )
    return part.reshape(shape[:lead] + (-1,) + shape[lead + 1 :])


def split_rows(field, lead):
    bits = bits_of("grp")
    shape = field.shape
    rows = shape[lead] >> len(bits)
    return field.reshape(shape[:lead] + (2,) * len(bits) + (rows,) + shape[lead + 1 :])


def halve(field, lead, bit):
    place = lead + bits_of("grp").index(bit)
    mine = flag_of("grp", bit)
    keep = lax.dynamic_index_in_dim(field, mine, place, keepdims=True)
    send = lax.dynamic_index_in_dim(field, 1 - mine, place, keepdims=True)
    return keep + swap(send.astype(bf16), "grp", bit).astype(f32)


def reduce_rows(field, lead):
    for bit in reversed(bits_of("grp")):
        field = halve(field, lead, bit)
    return field


def pass_on(pair):
    return pair[0] + swap(pair[1].astype(bf16), "tp", 2).astype(f32)


def per_device(
    tokens, grad_out, ln1_gain, ln1_shift, w_qkv, qkv_bias, rel_table, w_proj, proj_bias,
    ln2_gain, ln2_shift, w_in, in_bias, w_out, out_bias,
):
    groups, shares = lax.axis_size("grp"), lax.axis_size("tp")
    clips, local, width = tokens.shape
    move = Windows(clips, local, groups, shares)
    depth = w_qkv.shape[0]
    hidden = w_in.shape[1]
    heads = rel_table.shape[1]

    def own_share(field):
        return lax.dynamic_slice_in_dim(field, lax.axis_index("tp") * move.share, move.share, 0)

    split = jnp.concatenate([rel_table.T.reshape(-1), qkv_bias.reshape(-1), in_bias])
    split = jnp.stack([split, swap(split, "tp", 1)])
    split = jnp.concatenate([split, swap(split, "tp", 2)]).astype(f32)
    size = rel_table.size
    tables = split[:, :size].reshape(shares, heads, 1, TABLE)
    tables = jnp.pad(tables, ((0, 0), (0, 0), (0, 0), (0, TABLE_PAD - TABLE)))
    qkv_shift = split[:, size : size + qkv_bias.size].reshape(shares, 2, 1, GROUP)
    qkv_shift = jnp.concatenate(
        [qkv_shift[:, 0], jnp.zeros_like(qkv_shift[:, 0]), qkv_shift[:, 1]], axis=-1
    )
    in_shift = split[:, size + qkv_bias.size :][:, None]

    vectors = jnp.stack([ln1_gain, ln1_shift, proj_bias, ln2_gain, ln2_shift, out_bias])
    first = jnp.concatenate(
        [w_qkv.reshape(depth, 3 * GROUP), jnp.pad(vectors.T, ((0, 0), (0, GROUP - 6)))], axis=1
    )
    first = gather_over(first, "grp", 0)
    vectors = first[:, 3 * GROUP : 3 * GROUP + 6].T.astype(f32)
    gain_one, shift_one, proj_shift, gain_two, shift_two, out_shift = (
        vectors[i : i + 1] for i in range(6)
    )
    own = first[:, : 3 * GROUP]
    across = swap(own, "tp", 2)
    w_slots = [own, swap(own, "tp", 1), across, swap(across, "tp", 1)]

    x_rows = move.gather(own_share(tokens))

    home_in = gather_over(jnp.concatenate([w_in, w_proj], axis=1), "grp", 0)
    home_in = jnp.stack([home_in, swap(home_in, "tp", 2)])
    away_in = swap(home_in, "tp", 1)
    home_out = jnp.stack([w_out, swap(w_out, "tp", 2)])
    home_out = gather_over(home_out, "grp", 1)
    away_out = swap(home_out, "tp", 1)

    g_rows = move.gather(own_share(grad_out))

    pick = pick_matrix()
    ours, theirs = region_features(move.late, move.low)

    def bias_of(table):
        return pl.pallas_call(
            bias_kernel,
            out_shape=shaped((heads, PADDED, PADDED)),
            scratch_shapes=[
                pltpu.VMEM((heads, SIDE_PAD, TABLE_PAD), f32),
                pltpu.VMEM((heads, SIDE_PAD, DIAG_PAD), f32),
            ],
            compiler_params=PARAMS(),
            cost_estimate=cost(4.5),
            name="bias",
        )(table, pick)

    biases = [bias_of(tables[i]) for i in range(shares)]

    per_slot = [
        shaped((ROWS, 3 * GROUP), bf16),
        shaped((ROWS, GROUP), bf16),
        shaped((PAIR * heads, PADDED)),
    ]
    qkvs, o_parts, sums = [], [], []
    for i in range(shares):
        if i == 0:
            a1, a1_t, *made = pl.pallas_call(
                functools.partial(attention_kernel, True),
                out_shape=[shaped((ROWS, width), bf16), shaped((width, ROWS), bf16), *per_slot],
                compiler_params=PARAMS(),
                cost_estimate=cost(6),
                name="attention",
            )(x_rows, gain_one, shift_one, w_slots[i], qkv_shift[i], biases[i], ours, theirs)
        else:
            made = pl.pallas_call(
                functools.partial(attention_kernel, False),
                out_shape=per_slot,
                compiler_params=PARAMS(),
                cost_estimate=cost(5),
                name="attention",
            )(a1, w_slots[i], qkv_shift[i], biases[i], ours, theirs)
        qkvs.append(made[0])
        o_parts.append(made[1])
        sums.append(made[2])

    half = shares // 2
    rows, row = whole((ROWS, width)), whole((1, width))
    part = whole((ROWS, GROUP))
    in_block, out_block = whole((half, width, hidden + GROUP)), whole((half, width, hidden))
    proj_block = whole((half, width, GROUP))
    keep_spec = pl.BlockSpec((1, width, hidden), lambda i: (jnp.maximum(i - half, 0), 0, 0))
    send_spec = pl.BlockSpec((1, width, hidden), lambda i: (jnp.minimum(i, half - 1), 0, 0))
    unit_spec = pl.BlockSpec((1, 1, hidden), lambda i: (jnp.where(i < half, 2 * i + 1, 2 * i - shares), 0, 0))
    (
        out_rows, dh, dow, in_keep, in_send, out_keep, out_send, proj_keep, proj_send,
        grad_in_shift, vec_two,
    ) = pl.pallas_call(
        mlp_kernel,
        grid=(shares,),
        in_specs=[
            rows, part, part, part, part, rows, in_block, in_block, out_block, out_block,
            row, row, row, unit_spec, row,
        ],
        out_specs=[
            rows, rows, rows, keep_spec, send_spec, keep_spec, send_spec, proj_block, proj_block,
            unit_spec, whole((4, width)),
        ],
        out_shape=[
            shaped((ROWS, width), bf16),
            shaped((ROWS, width)),
            shaped((ROWS, width), bf16),
            shaped((half, width, hidden)),
            shaped((half, width, hidden), bf16),
            shaped((half, width, hidden)),
            shaped((half, width, hidden), bf16),
            shaped((half, width, GROUP)),
            shaped((half, width, GROUP), bf16),
            shaped((shares, 1, hidden)),
            shaped((4, width)),
        ],
        scratch_shapes=[
            pltpu.VMEM((ROWS, width), f32),
            pltpu.VMEM((ROWS, width), bf16),
            pltpu.VMEM((width, ROWS), bf16),
            pltpu.VMEM((width, ROWS), bf16),
            pltpu.VMEM((ROWS, width), f32),
            pltpu.VMEM((ROWS, 1), f32),
            pltpu.VMEM((ROWS, width), f32),
            pltpu.VMEM((ROWS, width), f32),
            pltpu.VMEM((ROWS, width), bf16),
            pltpu.VMEM((width, width), bf16),
            pltpu.VMEM((width, hidden), bf16),
            pltpu.VMEM((width, hidden), bf16),
        ],
        compiler_params=PARAMS(),
        cost_estimate=cost(22),
        name="mlp",
    )(
        x_rows, *o_parts, g_rows, home_in, away_in, home_out, away_out,
        proj_shift, gain_two, shift_two, in_shift, out_shift,
    )
    output = move.scatter(out_rows)

    got_out = out_keep + swap(out_send, "tp", 1).astype(f32)
    got_out = pass_on(got_out)
    got_out = reduce_rows(split_rows(got_out, 0), 0).reshape(depth, hidden)
    got_in = jnp.concatenate(
        [
            in_keep + swap(in_send, "tp", 1).astype(f32),
            proj_keep + swap(proj_send, "tp", 1).astype(f32),
        ],
        axis=-1,
    )
    got_in = reduce_rows(split_rows(got_in, 1), 1)
    got_in = pass_on(got_in).reshape(depth, hidden + GROUP)

    back = {}
    order = [1, 3, 0, 2]
    for i in order:
        first_call, last_call = i == order[0], i == order[-1]
        given = [a1_t, w_slots[i], qkvs[i], dow, sums[i], biases[i], ours, theirs]
        specs = [whole(v.shape) for v in given]
        specs[3] = pl.BlockSpec((ROWS, GROUP), functools.partial(lambda j, s: (0, j), i))
        if not first_call:
            given.append(running)
        if last_call:
            given += [x_rows, gain_one, dh]
        specs += [whole(v.shape) for v in given[8:]]
        made = [shaped((ROWS, width), bf16 if last_call else f32)]
        if last_call:
            made.append(shaped((2, width)))
        made += [
            shaped((width, 3 * GROUP), bf16 if i % 2 else f32),
            shaped((1, 3 * GROUP)),
            shaped((heads, PADDED, PADDED)),
        ]
        running, *made = pl.pallas_call(
            functools.partial(attention_back_kernel, first_call, last_call),
            grid=(1,),
            in_specs=specs,
            out_specs=[whole(v.shape) for v in made],
            out_shape=made,
            scratch_shapes=[pltpu.VMEM((ROWS, 3 * GROUP), bf16)],
            compiler_params=PARAMS(),
            cost_estimate=cost(9),
            name="attention_back",
        )(*given)
        if last_call:
            vec_one, *made = made
        back[i] = made
    grad_tokens = move.scatter(running).astype(f32)

    got_qkv = [back[i][0] + swap(back[i + 1][0], "tp", 1).astype(f32) for i in (0, 2)]
    got_qkv = pass_on(got_qkv)
    got_qkv = reduce_rows(split_rows(got_qkv, 0), 0).reshape(depth, 3, GROUP)

    def table_of(pair_sums):
        return pl.pallas_call(
            table_kernel,
            out_shape=shaped((heads, 1, TABLE_PAD)),
            scratch_shapes=[
                pltpu.VMEM((heads, SIDE_PAD, DIAG_PAD), f32),
                pltpu.VMEM((heads, SIDE_PAD, TABLE_PAD), f32),
            ],
            compiler_params=PARAMS(),
            cost_estimate=cost(4.5),
            name="table",
        )(pair_sums, pick)

    table_grads = {i: table_of(back[i][2]) for i in order}
    by_slot = [
        jnp.concatenate(
            [table_grads[i].reshape(-1), back[i][1].reshape(-1), grad_in_shift[i].reshape(-1)]
        ).reshape(-1, GROUP)
        for i in range(shares)
    ]
    vec = jnp.concatenate([vec_one, vec_two]).reshape(-1, GROUP)
    vec_size = vec.shape[0]
    kept = jnp.concatenate([vec, by_slot[0], by_slot[2]])
    kept = kept + swap(jnp.concatenate([vec, by_slot[1], by_slot[3]]), "tp", 1)
    cut = vec_size + by_slot[0].shape[0]
    rest = kept[:cut]
    small = rest + swap(jnp.concatenate([kept[:vec_size], kept[cut:]]), "tp", 2)
    for bit in reversed(bits_of("grp")):
        small = small + swap(small, "grp", bit)
    vec = small[:vec_size].reshape(6, width)
    vec = lax.dynamic_slice_in_dim(vec, lax.axis_index("grp") * depth, depth, 1)
    small = small[vec_size:].reshape(-1)
    got_table = small[: heads * TABLE_PAD].reshape(heads, TABLE_PAD)[:, :TABLE].T
    got_shift = small[heads * TABLE_PAD :][: 3 * GROUP].reshape(3, GROUP)
    got_in_shift = small[heads * TABLE_PAD + 3 * GROUP :]
    return (
        output,
        grad_tokens,
        vec[0],
        vec[1],
        got_qkv,
        jnp.stack([got_shift[0], got_shift[2]]),
        got_table,
        got_in[:, hidden:],
        vec[4],
        vec[2],
        vec[3],
        got_in[:, :hidden],
        got_in_shift,
        got_out,
        vec[5],
    )


def solution(mesh):
    shard = P("grp")
    tokens = P(None, "grp", None)
    placed = (
        tokens, tokens, shard, shard, P("grp", None, "tp"), P(None, "tp"), P(None, "tp"),
        P("grp", "tp"), shard, shard, shard, P("grp", "tp"), P("tp"), P("grp", "tp"), shard,
    )
    return jax.shard_map(
        per_device, mesh=mesh, in_specs=placed, out_specs=placed, check_vma=False
    )
```

time: 2400 us -> 400 us (0.17)
  other arithmetic: 1050 us -> 35.8 us
  local copies, waits for them, and re-layouts: 610 us -> 34.9 us
  blocking collectives: 332 us -> 0 us
  Pallas kernels: 0 us -> 160 us
  waiting for transfers between devices: 235 us -> 99.6 us
  matrix products: 132 us -> 0 us
  starting transfers between devices: 17.1 us -> 60.6 us
    scatter-add x1 -> x0, other arithmetic: 820 us -> none  [table_row(): return jax.ops.segment_sum(head_row, rel_places, num_segments=RB)]
    gather x1 -> x0, local copies, waits for them, and re-layouts: 281 us -> none  [per_device(): jnp.take(table_heads, rel_places, axis=1).reshape(head_local, WIN, WIN)]
    pallas_call x0 -> x17, Pallas kernels: none -> 160 us  [the longest x4 46.7 us: per_device(): pl.pallas_call(functools.partial(attention_back_kernel, first_call, last_...]
    all_gather x8 -> x0, blocking collectives: 155 us -> none  [the longest x1 36.8 us: per_device(): lax.all_gather(w_proj, 'grp', axis=0, tiled=True)]
    reduce_scatter x6 -> x0, waiting for transfers between devices: 134 us -> none  [the longest x1 51 us: per_device(): lax.psum_scatter(first_term, 'tp', scatter_dimension=0, tiled=True)]
    dot_general x40 -> x0, matrix products: 132 us -> none  [the longest x8 34.9 us: masked_scores(): jnp.einsum('wqhd,wkhd->whqk', query_b, key_b, preferred_element_type=jnp....]
    unnamed x2 -> x0, blocking collectives: 101 us -> none
    ppermute x0 -> x44, waiting for transfers between devices: none -> 99.6 us  [swap(): return lax.ppermute(field, axis, [(i, i ^ bit) for i in range(size)])]
  transfers between devices with their start and end apart: 14 -> 48, of which waited for: 6 -> 20; matrix products, arithmetic and copies ran while one was open for 56% -> 16% of each run, Pallas kernels for 0% -> 15%
where the time goes in v1:
time: 400 us; the launch traced here: 393 us
  Pallas kernels  160 us (40%)
  waiting for transfers between devices  99.6 us (25%)
  starting transfers between devices  60.6 us (15%)
  other arithmetic  35.8 us (9%)
  local copies, waits for them, and re-layouts  34.9 us (9%)
    ppermute x44, waiting for transfers between devices, swap(): return lax.ppermute(field, axis, [(i, i ^ bit) for i in range(size)])  99.6 us
    pallas_call x4, Pallas kernels, per_device(): pl.pallas_call(functools.partial(attention_back_kernel, first_call, last_...  46.7 us
    ppermute x44, starting transfers between devices, swap(): return lax.ppermute(field, axis, [(i, i ^ bit) for i in range(size)])  35.6 us
    pallas_call x4, Pallas kernels, bias_of(): pl.pallas_call(bias_kernel, out_shape=shaped((heads, PADDED, PADDED)), sc...  29.8 us
    pallas_call x4, Pallas kernels, table_of(): pl.pallas_call(table_kernel, out_shape=shaped((heads, 1, TABLE_PAD)), scr...  29.3 us
    all_to_all x4, starting transfers between devices, exchange(): lax.all_to_all(rows, 'grp', split_axis=0, concat_axis=0, tiled=True, axis...  25 us
    pallas_call x1, Pallas kernels, per_device(): pl.pallas_call(mlp_kernel, grid=(shares,), in_specs=[rows, part, part, pa...  24.2 us
    pallas_call x3, Pallas kernels, per_device(): pl.pallas_call(functools.partial(attention_kernel, False), out_shape=per_...  21.7 us
  transfers between devices with their start and end apart: 48, of which 20 were waited for; matrix products, arithmetic and copies ran while one was open for 16% of the time, Pallas kernels for 15%

profile of v1, /device:TPU:0, one launch (start us, length us, event | category | flops | bytes accessed | tf_op | source)
XLA Modules:
  0.0 392.8 jit_solution(15762800423079460115)
XLA Ops:
  0.7 3.0 collective-permute-start.13
  4.5 2.6 collective-permute-start.8
  14.6 7.1 %all-to-all-start = ((bf16[4,2,98,512]{3,1,2,0:T(2,128)(2,1)}), bf16[4,2,98,512]{3,1,2,0:T(2,128)(2,1)S(1)}, u32[]{:S(2)}, u32[]{:S(2)}) async-start(bf16[4,2,98,512]{3,1,2,0:T(2,128)(2,1)} %bitcast.4), calls=%async_computation | async-start | bytes 1605632 | tf_op jit(solution)/shard_map/all_to_all | solution.py:339
  26.1 2.5 fusion.pick_ref
  35.6 7.3 %bias.4.refs_5_.bias_ref = f32[4,400,400]{2,1,0:T(8,128)} custom-call(f32[4,1,2560]{2,1,0:T(1,128)} %get-tuple-element.186.table_ref, bf16[2560,768]{1,0:T(8,128)(2,1)} %fusion.pick_ref), custom_call_target="tpu_custom_call" | custom-call | flops 4950000128 | bytes 1048576 | tf_op jit(solution)/shard_map/bias/pallas_call | solution.py:490
  42.9 7.4 %bias.7.refs_3_.bias_ref = f32[4,400,400]{2,1,0:T(8,128)} custom-call(f32[4,1,2560]{2,1,0:T(1,128)} %get-tuple-element.183.table_ref, bf16[2560,768]{1,0:T(8,128)(2,1)} %fusion.pick_ref), custom_call_target="tpu_custom_call" | custom-call | flops 4950000128 | bytes 1048576 | tf_op jit(solution)/shard_map/bias/pallas_call | solution.py:490
  50.3 7.3 %bias.6.refs_3_.bias_ref = f32[4,400,400]{2,1,0:T(8,128)} custom-call(f32[4,1,2560]{2,1,0:T(1,128)} %get-tuple-element.185.table_ref, bf16[2560,768]{1,0:T(8,128)(2,1)} %fusion.pick_ref), custom_call_target="tpu_custom_call" | custom-call | flops 4950000128 | bytes 1048576 | tf_op jit(solution)/shard_map/bias/pallas_call | solution.py:490
  57.6 7.8 %bias.5.refs_3_.bias_ref = f32[4,400,400]{2,1,0:T(8,128)} custom-call(f32[4,1,2560]{2,1,0:T(1,128)} %get-tuple-element.184.table_ref, bf16[2560,768]{1,0:T(8,128)(2,1)} %fusion.pick_ref), custom_call_target="tpu_custom_call" | custom-call | flops 4950000128 | bytes 1048576 | tf_op jit(solution)/shard_map/bias/pallas_call | solution.py:490
  68.5 4.2 %collective-permute-done.14 = bf16[2,1,1,1,64,512]{5,4,0,3,2,1:T(8,128)(2,1)S(1)} collective-permute-done((bf16[2,1,1,1,64,512]{5,4,0,3,2,1:T(8,128)(2,1)S(1)}, bf16[2,1,1,1,64,512]{5,4,0,3,2,1:T(8,128)(2,1)S(1)}, u32[]{:S(2)}, u32[]{:S(2)}) %collective-permute-start.14) | collective-permute-done | bytes 131104 | tf_op jit(solution)/shard_map/ppermute | solution.py:386
  72.9 2.6 collective-permute-done.1
  77.1 1.9 collective-permute-done.9
  80.6 4.2 %collective-permute-done.2 = bf16[2,2,1,64,512]{4,3,2,1,0:T(8,128)(2,1)S(1)} collective-permute-done((bf16[2,2,1,64,512]{4,3,2,1,0:T(8,128)(2,1)S(1)}, bf16[2,2,1,64,512]{4,3,2,1,0:T(8,128)(2,1)S(1)}, u32[]{:S(2)}, u32[]{:S(2)}) %collective-permute-start.2) | collective-permute-done | bytes 262176 | tf_op jit(solution)/shard_map/ppermute | solution.py:386
  91.2 4.0 %collective-permute-done.6.refs_1_.w_ref = bf16[512,384]{1,0:T(8,128)(2,1)} collective-permute-done((bf16[512,384]{1,0:T(8,128)(2,1)}, bf16[512,384]{1,0:T(8,128)(2,1)}, u32[]{:S(2)}, u32[]{:S(2)}) %collective-permute-start.6) | collective-permute-done | bytes 393248 | tf_op jit(solution)/shard_map/ppermute | solution.py:386
  95.1 6.7 %collective-permute-done.16 = bf16[2,2,2,1,64,512]{5,4,0,3,2,1:T(8,128)(2,1)} collective-permute-done((bf16[2,2,2,1,64,512]{5,4,0,3,2,1:T(8,128)(2,1)}, bf16[2,2,2,1,64,512]{5,4,0,3,2,1:T(8,128)(2,1)}, u32[]{:S(2)}, u32[]{:S(2)}) %collective-permute-start.16) | collective-permute-done | bytes 524320 | tf_op jit(solution)/shard_map/ppermute | solution.py:386
  104.2 6.0 %all-to-all-start.1 = ((bf16[4,2,98,512]{3,1,2,0:T(2,128)(2,1)}), bf16[4,2,98,512]{3,1,2,0:T(2,128)(2,1)S(1)}, u32[]{:S(2)}, u32[]{:S(2)}) async-start(bf16[4,2,98,512]{3,1,2,0:T(2,128)(2,1)} %bitcast.35), calls=%async_computation.1 | async-start | bytes 1605632 | tf_op jit(solution)/shard_map/all_to_all | solution.py:339
  111.2 8.0 %attention.4 = (bf16[800,512]{1,0:T(8,128)(2,1)}, bf16[512,800]{1,0:T(8,128)(2,1)}, bf16[800,384]{1,0:T(8,128)(2,1)}, bf16[800,128]{1,0:T(8,128)(2,1)}, f32[8,400]{1,0:T(8,128)}) custom-call(bf16[800,512]{1,0:T(8,128)(2,1)} %bitcast.185, f32[1,512]{1,0:T(1,128)} %get-tuple-element.196.refs_1_.refs_2_, f32[1,512]{1,0:T(1,128)} %get-tuple-element.195.refs_2_, ...), custom_call_target="tpu_custom_call" | custom-call | flops 6600000000 | bytes 1048576 | tf_op jit(solution)/shard_map/attention/pallas_call | solution.py:512
  119.4 7.4 %attention.6 = (bf16[800,384]{1,0:T(8,128)(2,1)}, bf16[800,128]{1,0:T(8,128)(2,1)}, f32[8,400]{1,0:T(8,128)}) custom-call(bf16[800,512]{1,0:T(8,128)(2,1)} %get-tuple-element.58.refs_0_, bf16[512,384]{1,0:T(8,128)(2,1)} %collective-permute-done.6.refs_1_.w_ref, f32[1,384]{1,0:T(1,128)} %get-tuple-element.202.refs_2_, f32[4,400,400]{2,1,0:T(8,128)} %bias.6.refs_3_.bias_ref, ...), custom_call_target="tpu_custom_call" | custom-call | flops 5500000256 | bytes 1048576 | tf_op jit(solution)/shard_map/attention/pallas_call | solution.py:520
  127.9 7.0 %attention.5 = (bf16[800,384]{1,0:T(8,128)(2,1)}, bf16[800,128]{1,0:T(8,128)(2,1)}, f32[8,400]{1,0:T(8,128)}) custom-call(bf16[800,512]{1,0:T(8,128)(2,1)} %get-tuple-element.58.refs_0_, bf16[512,384]{1,0:T(8,128)(2,1)} %collective-permute-done.5.refs_1_.w_ref, f32[1,384]{1,0:T(1,128)} %get-tuple-element.203.refs_2_, f32[4,400,400]{2,1,0:T(8,128)} %bias.5.refs_3_.bias_ref, ...), custom_call_target="tpu_custom_call" | custom-call | flops 5500000256 | bytes 1048576 | tf_op jit(solution)/shard_map/attention/pallas_call | solution.py:520
  134.9 7.3 %attention.7 = (bf16[800,384]{1,0:T(8,128)(2,1)}, bf16[800,128]{1,0:T(8,128)(2,1)}, f32[8,400]{1,0:T(8,128)}) custom-call(bf16[800,512]{1,0:T(8,128)(2,1)} %get-tuple-element.58.refs_0_, bf16[512,384]{1,0:T(8,128)(2,1)} %collective-permute-done.7.refs_1_.w_ref, f32[1,384]{1,0:T(1,128)} %get-tuple-element.201.refs_2_, f32[4,400,400]{2,1,0:T(8,128)} %bias.7.refs_3_.bias_ref, ...), custom_call_target="tpu_custom_call" | custom-call | flops 5500000256 | bytes 1048576 | tf_op jit(solution)/shard_map/attention/pallas_call | solution.py:520
  143.3 24.2 %mlp.1 = (bf16[800,512]{1,0:T(8,128)(2,1)}, f32[800,512]{1,0:T(8,128)}, bf16[800,512]{1,0:T(8,128)(2,1)}, f32[2,512,512]{2,1,0:T(8,128)}, bf16[2,512,512]{2,1,0:...) custom-call(bf16[800,512]{1,0:T(8,128)(2,1)} %bitcast.186, ...), custom_call_target="tpu_custom_call" | custom-call | flops 24199999488 | bytes 1048576 | tf_op jit(solution)/shard_map/mlp/pallas_call | solution.py:542
  167.5 10.6 %attention_back.4 = (f32[800,512]{1,0:T(8,128)}, bf16[512,384]{1,0:T(8,128)(2,1)}, f32[1,384]{1,0:T(1,128)}, f32[4,400,400]{2,1,0:T(8,128)}) custom-call(bf16[512,800]{1,0:T(8,128)(2,1)} %get-tuple-element.63.a1_t_ref, bf16[512,384]{1,0:T(8,128)(2,1)} %collective-permute-done.5.refs_1_.w_ref, bf16[800,384]{1,0:T(8,128)(2,1)} %get-tuple-element.71.qkv_ref, ...), custom_call_target="tpu_custom_call" | custom-call | flops 9900000256 | bytes 1048576 | tf_op jit(solution)/shard_map/attention_back/pallas_call | solution.py:622
  178.0 11.3 %attention_back.5 = (f32[800,512]{1,0:T(8,128)}, bf16[512,384]{1,0:T(8,128)(2,1)}, f32[1,384]{1,0:T(1,128)}, f32[4,400,400]{2,1,0:T(8,128)}) custom-call(bf16[512,800]{1,0:T(8,128)(2,1)} %get-tuple-element.63.a1_t_ref, bf16[512,384]{1,0:T(8,128)(2,1)} %collective-permute-done.7.refs_1_.w_ref, bf16[800,384]{1,0:T(8,128)(2,1)} %get-tuple-element.69.qkv_ref, ...), custom_call_target="tpu_custom_call" | custom-call | flops 9900000256 | bytes 1048576 | tf_op jit(solution)/shard_map/attention_back/pallas_call | solution.py:622
  189.3 11.3 %attention_back.6 = (f32[800,512]{1,0:T(8,128)}, f32[512,384]{1,0:T(8,128)}, f32[1,384]{1,0:T(1,128)}, f32[4,400,400]{2,1,0:T(8,128)}) custom-call(bf16[512,800]{1,0:T(8,128)(2,1)} %get-tuple-element.63.a1_t_ref, bf16[512,384]{1,0:T(8,128)(2,1)} %slice.290.refs_3_.w_ref, bf16[800,384]{1,0:T(8,128)(2,1)} %get-tuple-element.67.qkv_ref, ...), custom_call_target="tpu_custom_call" | custom-call | flops 9900000256 | bytes 1048576 | tf_op jit(solution)/shard_map/attention_back/pallas_call | solution.py:622
  200.7 7.3 %table.4 = f32[4,1,2560]{2,1,0:T(1,128)} custom-call(f32[4,400,400]{2,1,0:T(8,128)} %get-tuple-element.80.sums_ref, bf16[2560,768]{1,0:T(8,128)(2,1)} %fusion.pick_ref), custom_call_target="tpu_custom_call" | custom-call | flops 4950000128 | bytes 1048576 | tf_op jit(solution)/shard_map/table/pallas_call | solution.py:643
  207.9 13.5 %attention_back.7 = (bf16[800,512]{1,0:T(8,128)(2,1)}, f32[2,512]{1,0:T(2,128)}, f32[512,384]{1,0:T(8,128)}, f32[1,384]{1,0:T(1,128)}, f32[4,400,400]{2,1,0:T(8,128)}) custom-call(bf16[512,800]{1,0:T(8,128)(2,1)} %get-tuple-element.63.a1_t_ref, bf16[512,384]{1,0:T(8,128)(2,1)} %collective-permute-done.6.refs_1_.w_ref, ...), custom_call_target="tpu_custom_call" | custom-call | flops 9900000256 | bytes 1048576 | tf_op jit(solution)/shard_map/attention_back/pallas_call | solution.py:622
  221.4 7.3 %table.5 = f32[4,1,2560]{2,1,0:T(1,128)} custom-call(f32[4,400,400]{2,1,0:T(8,128)} %get-tuple-element.83.sums_ref, bf16[2560,768]{1,0:T(8,128)(2,1)} %fusion.pick_ref), custom_call_target="tpu_custom_call" | custom-call | flops 4950000128 | bytes 1048576 | tf_op jit(solution)/shard_map/table/pallas_call | solution.py:643
  228.8 7.3 %table.6 = f32[4,1,2560]{2,1,0:T(1,128)} custom-call(f32[4,400,400]{2,1,0:T(8,128)} %get-tuple-element.85.sums_ref, bf16[2560,768]{1,0:T(8,128)(2,1)} %fusion.pick_ref), custom_call_target="tpu_custom_call" | custom-call | flops 4950000128 | bytes 1048576 | tf_op jit(solution)/shard_map/table/pallas_call | solution.py:643
  236.1 7.5 %table.7 = f32[4,1,2560]{2,1,0:T(1,128)} custom-call(f32[4,400,400]{2,1,0:T(8,128)} %get-tuple-element.87.sums_ref, bf16[2560,768]{1,0:T(8,128)(2,1)} %fusion.pick_ref), custom_call_target="tpu_custom_call" | custom-call | flops 4950000128 | bytes 1048576 | tf_op jit(solution)/shard_map/table/pallas_call | solution.py:643
  247.5 2.7 collective-permute-done.23
  251.7 2.7 collective-permute-done.24
  254.5 2.1 collective-permute-start.25
  258.7 6.0 %all-to-all-start.3 = ((bf16[4,2,98,512]{3,1,2,0:T(2,128)(2,1)}), bf16[4,2,98,512]{3,1,2,0:T(2,128)(2,1)S(1)}, u32[]{:S(2)}, u32[]{:S(2)}) async-start(bf16[4,2,98,512]{3,1,2,0:T(2,128)(2,1)} %bitcast.57), calls=%async_computation.3 | async-start | bytes 1605632 | tf_op jit(solution)/shard_map/all_to_all | solution.py:339
  266.4 1.9 convert_add_fusion.6
  268.3 16.5 %collective-permute-done.26 = f32[111,128]{1,0:T(8,128)S(1)} collective-permute-done((f32[111,128]{1,0:T(8,128)S(1)}, f32[111,128]{1,0:T(8,128)S(1)}, u32[]{:S(2)}, u32[]{:S(2)}) %collective-permute-start.26) | collective-permute-done | bytes 56864 | tf_op jit(solution)/shard_map/ppermute | solution.py:386
  290.4 8.3 %collective-permute-done.29 = bf16[512,384]{1,0:T(8,128)(2,1)S(1)} collective-permute-done((bf16[512,384]{1,0:T(8,128)(2,1)S(1)}, bf16[512,384]{1,0:T(8,128)(2,1)S(1)}, u32[]{:S(2)}, u32[]{:S(2)}) %collective-permute-start.29) | collective-permute-done | bytes 393248 | tf_op jit(solution)/shard_map/ppermute | solution.py:386
  302.0 3.6 collective-permute-done.30
  310.3 5.9 %all-to-all-start.2 = ((bf16[4,2,98,512]{3,1,2,0:T(2,128)(2,1)}), bf16[4,2,98,512]{3,1,2,0:T(2,128)(2,1)}, u32[]{:S(2)}, u32[]{:S(2)}) async-start(bf16[4,2,98,512]{3,1,2,0:T(2,128)(2,1)} %bitcast.49), calls=%async_computation.2 | async-start | bytes 1605632 | tf_op jit(solution)/shard_map/all_to_all | solution.py:339
  323.4 11.0 %collective-permute-done.32 = bf16[1,1,1,64,384]{4,3,2,1,0:T(8,128)(2,1)S(1)} collective-permute-done((bf16[1,1,1,64,384]{4,3,2,1,0:T(8,128)(2,1)S(1)}, bf16[1,1,1,64,384]{4,3,2,1,0:T(8,128)(2,1)S(1)}, u32[]{:S(2)}, u32[]{:S(2)}) %collective-permute-start.32) | collective-permute-done | bytes 49184 | tf_op jit(solution)/shard_map/ppermute | solution.py:386
  337.9 1.8 copy.135
  343.9 1.8 collective-permute-start.41
  349.2 2.7 collective-permute-done.41
  353.4 2.1 collective-permute-start.36
  355.5 3.1 collective-permute-done.42
  358.7 4.3 %collective-permute-done.20 = bf16[1,1,2,392,512]{4,3,2,1,0:T(8,128)(2,1)S(1)} collective-permute-done((bf16[1,1,2,392,512]{4,3,2,1,0:T(8,128)(2,1)S(1)}, bf16[1,1,2,392,512]{4,3,2,1,0:T(8,128)(2,1)S(1)}, u32[]{:S(2)}, u32[]{:S(2)}) %collective-permute-start.20) | collective-permute-done | bytes 802848 | tf_op jit(solution)/shard_map/ppermute | solution.py:386
  365.0 14.2 %collective-permute-done.18 = bf16[1,1,2,392,512]{4,3,2,1,0:T(8,128)(2,1)S(1)} collective-permute-done((bf16[1,1,2,392,512]{4,3,2,1,0:T(8,128)(2,1)S(1)}, bf16[1,1,2,392,512]{4,3,2,1,0:T(8,128)(2,1)S(1)}, u32[]{:S(2)}, u32[]{:S(2)}) %collective-permute-start.18) | collective-permute-done | bytes 802848 | tf_op jit(solution)/shard_map/ppermute | solution.py:386
  380.9 3.7 collective-permute-done.38
  386.4 3.9 bitcast_convert_fusion
  390.5 2.0 pad_maximum_fusion
  (294 shorter events, 86.0 us)
Async XLA Ops:
  0.7 65.4 %collective-permute-start.13 = (bf16[64,512]{1,0:T(8,128)(2,1)}, bf16[64,512]{1,0:T(8,128)(2,1)S(1)}, u32[]{:S(2)}, u32[]{:S(2)}) collective-permute-start(bf16[64,512]{1,0:T(8,128)(2,1)} %param.28), channel_id=1, source_target_pairs={{0,2},{1,3},{2,0},{3,1},{4,6},{5,7},{6,4},{7,5},{8,10},{9,11},{10,... | collective-permute-start | bytes 196616 | tf_op jit(solution)/shard_map/ppermute | solution.py:386
  4.5 62.4 %collective-permute-start.8 = (bf16[1,1,1,64,640]{4,3,2,1,0:T(8,128)(2,1)S(1)}, bf16[1,1,1,64,640]{4,3,2,1,0:T(8,128)(2,1)S(1)}, u32[]{:S(2)}, u32[]{:S(2)}) collective-permute-start(bf16[1,1,1,64,640]{4,3,2,1,0:T(8,128)(2,1)S(1)} %maximum_bitcast_fusion.1), channel_id=1, source_target_pairs={{0,16},{4,20},{8,24},{12,28},{16,0},{20,4},{24,8},{28,12},{1,17},{... | collective-permute-start | bytes 245768 | tf_op jit(solution)/shard_map/ppermute | solution.py:386
  8.1 58.1 %collective-permute-start = (bf16[1,1,1,64,512]{4,3,2,1,0:T(8,128)(2,1)S(1)}, bf16[1,1,1,64,512]{4,3,2,1,0:T(8,128)(2,1)S(1)}, u32[]{:S(2)}, u32[]{:S(2)}) collective-permute-start(bf16[1,1,1,64,512]{4,3,2,1,0:T(8,128)(2,1)S(1)} %fusion.26), channel_id=1, source_target_pairs={{0,16},{4,20},{8,24},{12,28},{16,0},{20,4},{24,8},{28,12},{1,17},{... | collective-permute-start | bytes 196616 | tf_op jit(solution)/shard_map/ppermute | solution.py:386
  14.6 89.5 %all-to-all-start = ((bf16[4,2,98,512]{3,1,2,0:T(2,128)(2,1)}), bf16[4,2,98,512]{3,1,2,0:T(2,128)(2,1)S(1)}, u32[]{:S(2)}, u32[]{:S(2)}) async-start(bf16[4,2,98,512]{3,1,2,0:T(2,128)(2,1)} %bitcast.4), calls=%async_computation | async-start | bytes 1605632 | tf_op jit(solution)/shard_map/all_to_all | solution.py:339
  21.9 7.5 %collective-permute-start.3 = (bf16[10908]{0:T(1024)(128)(2,1)S(1)}, bf16[10908]{0:T(1024)(128)(2,1)S(1)}, u32[]{:S(2)}, u32[]{:S(2)}) collective-permute-start(bf16[10908]{0:T(1024)(128)(2,1)S(1)} %concatenate.116), channel_id=1, source_target_pairs={{0,1},{1,0},{2,3},{3,2},{4,5},{5,4},{6,7},{7,6},{8,9},{9,8},{10,11... | collective-permute-start | bytes 65456 | tf_op jit(solution)/shard_map/ppermute | solution.py:386
  29.6 4.1 %collective-permute-start.4 = (bf16[2,10908]{1,0:T(2,128)(2,1)S(1)}, bf16[2,10908]{1,0:T(2,128)(2,1)S(1)}, u32[]{:S(2)}, u32[]{:S(2)}) collective-permute-start(bf16[2,10908]{1,0:T(2,128)(2,1)S(1)} %pad_maximum_fusion.24), channel_id=1, source_target_pairs={{0,2},{1,3},{2,0},{3,1},{4,6},{5,7},{6,4},{7,5},{8,10},{9,11},{10,... | collective-permute-start | bytes 130904 | tf_op jit(solution)/shard_map/ppermute | solution.py:386
  66.1 6.6 %collective-permute-start.14 = (bf16[2,1,1,1,64,512]{5,4,0,3,2,1:T(8,128)(2,1)S(1)}, bf16[2,1,1,1,64,512]{5,4,0,3,2,1:T(8,128)(2,1)S(1)}, u32[]{:S(2)}, u32[]{:S(2)}) collective-permute-start(bf16[2,1,1,1,64,512]{5,4,0,3,2,1:T(8,128)(2,1)S(1)} %maximum_bitcast_fusion), channel_id=1, source_target_pairs={{0,16},{4,20},{8,24},{12,28},{16,0},{20,4},{24,8},{28,12},{1,17},{... | collective-permute-start | bytes 393224 | tf_op jit(solution)/shard_map/ppermute | solution.py:386
  66.3 9.2 %collective-permute-start.1 = (bf16[2,1,1,64,512]{4,3,2,1,0:T(8,128)(2,1)S(1)}, bf16[2,1,1,64,512]{4,3,2,1,0:T(8,128)(2,1)S(1)}, u32[]{:S(2)}, u32[]{:S(2)}) collective-permute-start(bf16[2,1,1,64,512]{4,3,2,1,0:T(8,128)(2,1)S(1)} %pad_maximum_fusion.22), channel_id=1, source_target_pairs={{0,8},{4,12},{8,0},{12,4},{16,24},{20,28},{24,16},{28,20},{1,9},{5... | collective-permute-start | bytes 393224 | tf_op jit(solution)/shard_map/ppermute | solution.py:386
  67.0 12.0 %collective-permute-start.9 = (bf16[2,1,1,64,640]{4,3,2,1,0:T(8,128)(2,1)S(1)}, bf16[2,1,1,64,640]{4,3,2,1,0:T(8,128)(2,1)S(1)}, u32[]{:S(2)}, u32[]{:S(2)}) collective-permute-start(bf16[2,1,1,64,640]{4,3,2,1,0:T(8,128)(2,1)S(1)} %pad_maximum_fusion.19), channel_id=1, source_target_pairs={{0,8},{4,12},{8,0},{12,4},{16,24},{20,28},{24,16},{28,20},{1,9},{5... | collective-permute-start | bytes 491528 | tf_op jit(solution)/shard_map/ppermute | solution.py:386
  72.8 13.6 %collective-permute-start.15 = (bf16[2,2,1,1,64,512]{5,4,0,3,2,1:T(8,128)(2,1)S(1)}, bf16[2,2,1,1,64,512]{5,4,0,3,2,1:T(8,128)(2,1)S(1)}, u32[]{:S(2)}, u32[]{:S(2)}) collective-permute-start(bf16[2,2,1,1,64,512]{5,4,0,3,2,1:T(8,128)(2,1)S(1)} %pad_maximum_fusion.18), channel_id=1, source_target_pairs={{0,8},{4,12},{8,0},{12,4},{16,24},{20,28},{24,16},{28,20},{1,9},{5... | collective-permute-start | bytes 786440 | tf_op jit(solution)/shard_map/ppermute | solution.py:386
  75.6 9.2 %collective-permute-start.2 = (bf16[2,2,1,64,512]{4,3,2,1,0:T(8,128)(2,1)S(1)}, bf16[2,2,1,64,512]{4,3,2,1,0:T(8,128)(2,1)S(1)}, u32[]{:S(2)}, u32[]{:S(2)}) collective-permute-start(bf16[2,2,1,64,512]{4,3,2,1,0:T(8,128)(2,1)S(1)} %pad_maximum_fusion.17), channel_id=1, source_target_pairs={{0,4},{4,0},{8,12},{12,8},{16,20},{20,16},{24,28},{28,24},{1,5},{5... | collective-permute-start | bytes 786440 | tf_op jit(solution)/shard_map/ppermute | solution.py:386
  79.1 10.3 %collective-permute-start.10 = (bf16[2,2,1,64,640]{4,3,2,1,0:T(8,128)(2,1)S(1)}, bf16[2,2,1,64,640]{4,3,2,1,0:T(8,128)(2,1)S(1)}, u32[]{:S(2)}, u32[]{:S(2)}) collective-permute-start(bf16[2,2,1,64,640]{4,3,2,1,0:T(8,128)(2,1)S(1)} %pad_maximum_fusion.16), channel_id=1, source_target_pairs={{0,4},{4,0},{8,12},{12,8},{16,20},{20,16},{24,28},{28,24},{1,5},{5... | collective-permute-start | bytes 983048 | tf_op jit(solution)/shard_map/ppermute | solution.py:386
  85.7 9.4 %collective-permute-start.6 = (bf16[512,384]{1,0:T(8,128)(2,1)}, bf16[512,384]{1,0:T(8,128)(2,1)}, u32[]{:S(2)}, u32[]{:S(2)}) collective-permute-start(bf16[512,384]{1,0:T(8,128)(2,1)} %slice.290.refs_3_.w_ref), channel_id=1, source_target_pairs={{0,2},{1,3},{2,0},{3,1},{4,6},{5,7},{6,4},{7,5},{8,10},{9,11},{10,... | collective-permute-start | bytes 1179656 | tf_op jit(solution)/shard_map/ppermute | solution.py:386
  86.3 41.6 %collective-permute-start.5 = (bf16[512,384]{1,0:T(8,128)(2,1)}, bf16[512,384]{1,0:T(8,128)(2,1)}, u32[]{:S(2)}, u32[]{:S(2)}) collective-permute-start(bf16[512,384]{1,0:T(8,128)(2,1)} %slice.290.refs_3_.w_ref), channel_id=1, source_target_pairs={{0,1},{1,0},{2,3},{3,2},{4,5},{5,4},{6,7},{7,6},{8,9},{9,8},{10,11... | collective-permute-start | bytes 1179656 | tf_op jit(solution)/shard_map/ppermute | solution.py:386
  87.2 14.7 %collective-permute-start.16 = (bf16[2,2,2,1,64,512]{5,4,0,3,2,1:T(8,128)(2,1)}, bf16[2,2,2,1,64,512]{5,4,0,3,2,1:T(8,128)(2,1)}, u32[]{:S(2)}, u32[]{:S(2)}) collective-permute-start(bf16[2,2,2,1,64,512]{5,4,0,3,2,1:T(8,128)(2,1)} %pad_maximum_fusion.15), channel_id=1, source_target_pairs={{0,4},{4,0},{8,12},{12,8},{16,20},{20,16},{24,28},{28,24},{1,5},{5... | collective-permute-start | bytes 1572872 | tf_op jit(solution)/shard_map/ppermute | solution.py:386
  89.6 29.6 %collective-permute-start.11 = (bf16[512,640]{1,0:T(8,128)(2,1)S(1)}, bf16[512,640]{1,0:T(8,128)(2,1)S(1)}, u32[]{:S(2)}, u32[]{:S(2)}) collective-permute-start(bf16[512,640]{1,0:T(8,128)(2,1)S(1)} %bitcast.179), channel_id=1, source_target_pairs={{0,2},{1,3},{2,0},{3,1},{4,6},{5,7},{6,4},{7,5},{8,10},{9,11},{10,... | collective-permute-start | bytes 1966088 | tf_op jit(solution)/shard_map/ppermute | solution.py:386
  95.1 39.8 %collective-permute-start.7 = (bf16[512,384]{1,0:T(8,128)(2,1)}, bf16[512,384]{1,0:T(8,128)(2,1)}, u32[]{:S(2)}, u32[]{:S(2)}) collective-permute-start(bf16[512,384]{1,0:T(8,128)(2,1)} %collective-permute-done.6.refs_1_.w_ref), channel_id=1, source_target_pairs={{0,1},{1,0},{2,3},{3,2},{4,5},{5,4},{6,7},{7,6},{8,9},{9,8},{10,11... | collective-permute-start | bytes 1179656 | tf_op jit(solution)/shard_map/ppermute | solution.py:386
  104.2 38.0 %collective-permute-start.17 = (bf16[2,512,512]{2,1,0:T(8,128)(2,1)}, bf16[2,512,512]{2,1,0:T(8,128)(2,1)}, u32[]{:S(2)}, u32[]{:S(2)}) collective-permute-start(bf16[2,512,512]{2,1,0:T(8,128)(2,1)} %bitcast.46.home_out), channel_id=1, source_target_pairs={{0,1},{1,0},{2,3},{3,2},{4,5},{5,4},{6,7},{7,6},{8,9},{9,8},{10,11... | collective-permute-start | bytes 3145736 | tf_op jit(solution)/shard_map/ppermute | solution.py:386
  104.2 22.7 %all-to-all-start.1 = ((bf16[4,2,98,512]{3,1,2,0:T(2,128)(2,1)}), bf16[4,2,98,512]{3,1,2,0:T(2,128)(2,1)S(1)}, u32[]{:S(2)}, u32[]{:S(2)}) async-start(bf16[4,2,98,512]{3,1,2,0:T(2,128)(2,1)} %bitcast.35), calls=%async_computation.1 | async-start | bytes 1605632 | tf_op jit(solution)/shard_map/all_to_all | solution.py:339
  119.4 22.9 %collective-permute-start.12 = (bf16[2,512,640]{2,1,0:T(8,128)(2,1)S(1)}, bf16[2,512,640]{2,1,0:T(8,128)(2,1)S(1)}, u32[]{:S(2)}, u32[]{:S(2)}) collective-permute-start(bf16[2,512,640]{2,1,0:T(8,128)(2,1)S(1)} %pad_maximum_fusion.5.home_in), channel_id=1, source_target_pairs={{0,1},{1,0},{2,3},{3,2},{4,5},{5,4},{6,7},{7,6},{8,9},{9,8},{10,11... | collective-permute-start | bytes 3932168 | tf_op jit(solution)/shard_map/ppermute | solution.py:386
  244.5 1.4 collective-permute-start.22
  246.0 4.2 %collective-permute-start.23 = (f32[111,128]{1,0:T(8,128)S(1)}, f32[111,128]{1,0:T(8,128)S(1)}, u32[]{:S(2)}, u32[]{:S(2)}) collective-permute-start(f32[111,128]{1,0:T(8,128)S(1)} %pad_maximum_fusion.23), channel_id=1, source_target_pairs={{0,2},{1,3},{2,0},{3,1},{4,6},{5,7},{6,4},{7,5},{8,10},{9,11},{10,... | collective-permute-start | bytes 170504 | tf_op jit(solution)/shard_map/ppermute | solution.py:386
  247.5 18.7 %collective-permute-start.34 = (bf16[2,512,128]{2,1,0:T(8,128)(2,1)}, bf16[2,512,128]{2,1,0:T(8,128)(2,1)}, u32[]{:S(2)}, u32[]{:S(2)}) collective-permute-start(bf16[2,512,128]{2,1,0:T(8,128)(2,1)} %get-tuple-element.96), channel_id=1, source_target_pairs={{0,1},{1,0},{2,3},{3,2},{4,5},{5,4},{6,7},{7,6},{8,9},{9,8},{10,11... | collective-permute-start | bytes 786440 | tf_op jit(solution)/shard_map/ppermute | solution.py:386
  250.2 4.2 %collective-permute-start.24 = (f32[111,128]{1,0:T(8,128)S(1)}, f32[111,128]{1,0:T(8,128)S(1)}, u32[]{:S(2)}, u32[]{:S(2)}) collective-permute-start(f32[111,128]{1,0:T(8,128)S(1)} %slice_add_fusion), channel_id=1, source_target_pairs={{0,4},{4,0},{8,12},{12,8},{16,20},{20,16},{24,28},{28,24},{1,5},{5... | collective-permute-start | bytes 170504 | tf_op jit(solution)/shard_map/ppermute | solution.py:386
  254.5 11.8 %collective-permute-start.25 = (f32[111,128]{1,0:T(8,128)S(1)}, f32[111,128]{1,0:T(8,128)S(1)}, u32[]{:S(2)}, u32[]{:S(2)}) collective-permute-start(f32[111,128]{1,0:T(8,128)S(1)} %add.228), channel_id=1, source_target_pairs={{0,8},{4,12},{8,0},{12,4},{16,24},{20,28},{24,16},{28,20},{1,9},{5... | collective-permute-start | bytes 170504 | tf_op jit(solution)/shard_map/ppermute | solution.py:386
  256.6 49.1 %collective-permute-start.39 = (bf16[2,512,512]{2,1,0:T(8,128)(2,1)}, bf16[2,512,512]{2,1,0:T(8,128)(2,1)S(1)}, u32[]{:S(2)}, u32[]{:S(2)}) collective-permute-start(bf16[2,512,512]{2,1,0:T(8,128)(2,1)} %get-tuple-element.98), channel_id=1, source_target_pairs={{0,1},{1,0},{2,3},{3,2},{4,5},{5,4},{6,7},{7,6},{8,9},{9,8},{10,11... | collective-permute-start | bytes 3145736 | tf_op jit(solution)/shard_map/ppermute | solution.py:386
  256.6 59.7 %collective-permute-start.33 = (bf16[2,512,512]{2,1,0:T(8,128)(2,1)}, bf16[2,512,512]{2,1,0:T(8,128)(2,1)}, u32[]{:S(2)}, u32[]{:S(2)}) collective-permute-start(bf16[2,512,512]{2,1,0:T(8,128)(2,1)} %get-tuple-element.94), channel_id=1, source_target_pairs={{0,1},{1,0},{2,3},{3,2},{4,5},{5,4},{6,7},{7,6},{8,9},{9,8},{10,11... | collective-permute-start | bytes 3145736 | tf_op jit(solution)/shard_map/ppermute | solution.py:386
  257.1 29.8 %collective-permute-start.28 = (bf16[512,384]{1,0:T(8,128)(2,1)}, bf16[512,384]{1,0:T(8,128)(2,1)}, u32[]{:S(2)}, u32[]{:S(2)}) collective-permute-start(bf16[512,384]{1,0:T(8,128)(2,1)} %get-tuple-element.92), channel_id=1, source_target_pairs={{0,1},{1,0},{2,3},{3,2},{4,5},{5,4},{6,7},{7,6},{8,9},{9,8},{10,11... | collective-permute-start | bytes 1179656 | tf_op jit(solution)/shard_map/ppermute | solution.py:386
  258.7 51.6 %all-to-all-start.3 = ((bf16[4,2,98,512]{3,1,2,0:T(2,128)(2,1)}), bf16[4,2,98,512]{3,1,2,0:T(2,128)(2,1)S(1)}, u32[]{:S(2)}, u32[]{:S(2)}) async-start(bf16[4,2,98,512]{3,1,2,0:T(2,128)(2,1)} %bitcast.57), calls=%async_computation.3 | async-start | bytes 1605632 | tf_op jit(solution)/shard_map/all_to_all | solution.py:339
  266.2 24.2 %collective-permute-start.27 = (bf16[512,384]{1,0:T(8,128)(2,1)}, bf16[512,384]{1,0:T(8,128)(2,1)}, u32[]{:S(2)}, u32[]{:S(2)}) collective-permute-start(bf16[512,384]{1,0:T(8,128)(2,1)} %get-tuple-element.90), channel_id=1, source_target_pairs={{0,1},{1,0},{2,3},{3,2},{4,5},{5,4},{6,7},{7,6},{8,9},{9,8},{10,11... | collective-permute-start | bytes 1179656 | tf_op jit(solution)/shard_map/ppermute | solution.py:386
  266.3 18.5 %collective-permute-start.26 = (f32[111,128]{1,0:T(8,128)S(1)}, f32[111,128]{1,0:T(8,128)S(1)}, u32[]{:S(2)}, u32[]{:S(2)}) collective-permute-start(f32[111,128]{1,0:T(8,128)S(1)} %add.229), channel_id=1, source_target_pairs={{0,16},{4,20},{8,24},{12,28},{16,0},{20,4},{24,8},{28,12},{1,17},{... | collective-permute-start | bytes 170504 | tf_op jit(solution)/shard_map/ppermute | solution.py:386
  288.0 10.7 %collective-permute-start.29 = (bf16[512,384]{1,0:T(8,128)(2,1)S(1)}, bf16[512,384]{1,0:T(8,128)(2,1)S(1)}, u32[]{:S(2)}, u32[]{:S(2)}) collective-permute-start(bf16[512,384]{1,0:T(8,128)(2,1)S(1)} %add_convert_fusion), channel_id=1, source_target_pairs={{0,2},{1,3},{2,0},{3,1},{4,6},{5,7},{6,4},{7,5},{8,10},{9,11},{10,... | collective-permute-start | bytes 1179656 | tf_op jit(solution)/shard_map/ppermute | solution.py:386
  299.8 5.7 %collective-permute-start.30 = (bf16[2,2,1,64,384]{4,3,2,1,0:T(8,128)(2,1)S(1)}, bf16[2,2,1,64,384]{4,3,2,1,0:T(8,128)(2,1)S(1)}, u32[]{:S(2)}, u32[]{:S(2)}) collective-permute-start(bf16[2,2,1,64,384]{4,3,2,1,0:T(8,128)(2,1)S(1)} %dynamic-slice_convert_fusion.3), channel_id=1, source_target_pairs={{0,4},{4,0},{8,12},{12,8},{16,20},{20,16},{24,28},{28,24},{1,5},{5... | collective-permute-start | bytes 589832 | tf_op jit(solution)/shard_map/ppermute | solution.py:386
  305.7 12.5 %collective-permute-start.31 = (bf16[2,1,1,64,384]{4,3,2,1,0:T(8,128)(2,1)S(1)}, bf16[2,1,1,64,384]{4,3,2,1,0:T(8,128)(2,1)}, u32[]{:S(2)}, u32[]{:S(2)}) collective-permute-start(bf16[2,1,1,64,384]{4,3,2,1,0:T(8,128)(2,1)S(1)} %dynamic-slice_convert_fusion.6), channel_id=1, source_target_pairs={{0,8},{4,12},{8,0},{12,4},{16,24},{20,28},{24,16},{28,20},{1,9},{5... | collective-permute-start | bytes 294920 | tf_op jit(solution)/shard_map/ppermute | solution.py:386
  308.9 33.7 %collective-permute-start.40 = (bf16[512,512]{1,0:T(8,128)(2,1)}, bf16[512,512]{1,0:T(8,128)(2,1)}, u32[]{:S(2)}, u32[]{:S(2)}) collective-permute-start(bf16[512,512]{1,0:T(8,128)(2,1)} %fusion.8), channel_id=1, source_target_pairs={{0,2},{1,3},{2,0},{3,1},{4,6},{5,7},{6,4},{7,5},{8,10},{9,11},{10,... | collective-permute-start | bytes 1572872 | tf_op jit(solution)/shard_map/ppermute | solution.py:386
  310.3 27.5 %all-to-all-start.2 = ((bf16[4,2,98,512]{3,1,2,0:T(2,128)(2,1)}), bf16[4,2,98,512]{3,1,2,0:T(2,128)(2,1)}, u32[]{:S(2)}, u32[]{:S(2)}) async-start(bf16[4,2,98,512]{3,1,2,0:T(2,128)(2,1)} %bitcast.49), calls=%async_computation.2 | async-start | bytes 1605632 | tf_op jit(solution)/shard_map/all_to_all | solution.py:339
  319.8 14.6 %collective-permute-start.32 = (bf16[1,1,1,64,384]{4,3,2,1,0:T(8,128)(2,1)S(1)}, bf16[1,1,1,64,384]{4,3,2,1,0:T(8,128)(2,1)S(1)}, u32[]{:S(2)}, u32[]{:S(2)}) collective-permute-start(bf16[1,1,1,64,384]{4,3,2,1,0:T(8,128)(2,1)S(1)} %dynamic-slice_convert_fusion.8), channel_id=1, source_target_pairs={{0,16},{4,20},{8,24},{12,28},{16,0},{20,4},{24,8},{28,12},{1,17},{... | collective-permute-start | bytes 147464 | tf_op jit(solution)/shard_map/ppermute | solution.py:386
  321.9 30.2 %collective-permute-start.35 = (bf16[2,2,2,1,64,640]{5,4,3,2,1,0:T(8,128)(2,1)}, bf16[2,2,2,1,64,640]{5,4,3,2,1,0:T(8,128)(2,1)}, u32[]{:S(2)}, u32[]{:S(2)}) collective-permute-start(bf16[2,2,2,1,64,640]{5,4,3,2,1,0:T(8,128)(2,1)} %dynamic-slice_convert_fusion), channel_id=1, source_target_pairs={{0,4},{4,0},{8,12},{12,8},{16,20},{20,16},{24,28},{28,24},{1,5},{5... | collective-permute-start | bytes 1966088 | tf_op jit(solution)/shard_map/ppermute | solution.py:386
  342.1 20.8 %collective-permute-start.20 = (bf16[1,1,2,392,512]{4,3,2,1,0:T(8,128)(2,1)S(1)}, bf16[1,1,2,392,512]{4,3,2,1,0:T(8,128)(2,1)S(1)}, u32[]{:S(2)}, u32[]{:S(2)}) collective-permute-start(bf16[1,1,2,392,512]{4,3,2,1,0:T(8,128)(2,1)S(1)} %copy.143), channel_id=1, source_target_pairs={{0,2},{1,3},{2,0},{3,1},{4,6},{5,7},{6,4},{7,5},{8,10},{9,11},{10,... | collective-permute-start | bytes 2408456 | tf_op jit(solution)/shard_map/ppermute | solution.py:386
  343.9 8.0 %collective-permute-start.41 = (bf16[2,2,1,64,512]{4,3,2,1,0:T(8,128)(2,1)S(1)}, bf16[2,2,1,64,512]{4,3,2,1,0:T(8,128)(2,1)S(1)}, u32[]{:S(2)}, u32[]{:S(2)}) collective-permute-start(bf16[2,2,1,64,512]{4,3,2,1,0:T(8,128)(2,1)S(1)} %dynamic-slice_convert_fusion.2), channel_id=1, source_target_pairs={{0,4},{4,0},{8,12},{12,8},{16,20},{20,16},{24,28},{28,24},{1,5},{5... | collective-permute-start | bytes 786440 | tf_op jit(solution)/shard_map/ppermute | solution.py:386
  347.6 31.6 %collective-permute-start.18 = (bf16[1,1,2,392,512]{4,3,2,1,0:T(8,128)(2,1)S(1)}, bf16[1,1,2,392,512]{4,3,2,1,0:T(8,128)(2,1)S(1)}, u32[]{:S(2)}, u32[]{:S(2)}) collective-permute-start(bf16[1,1,2,392,512]{4,3,2,1,0:T(8,128)(2,1)S(1)} %copy.137), channel_id=1, source_target_pairs={{0,2},{1,3},{2,0},{3,1},{4,6},{5,7},{6,4},{7,5},{8,10},{9,11},{10,... | collective-permute-start | bytes 2408456 | tf_op jit(solution)/shard_map/ppermute | solution.py:386
  352.0 6.5 %collective-permute-start.42 = (bf16[2,1,1,64,512]{4,3,2,1,0:T(8,128)(2,1)S(1)}, bf16[2,1,1,64,512]{4,3,2,1,0:T(8,128)(2,1)S(1)}, u32[]{:S(2)}, u32[]{:S(2)}) collective-permute-start(bf16[2,1,1,64,512]{4,3,2,1,0:T(8,128)(2,1)S(1)} %dynamic-slice_convert_fusion.5), channel_id=1, source_target_pairs={{0,8},{4,12},{8,0},{12,4},{16,24},{20,28},{24,16},{28,20},{1,9},{5... | collective-permute-start | bytes 393224 | tf_op jit(solution)/shard_map/ppermute | solution.py:386
  353.4 11.4 %collective-permute-start.36 = (bf16[2,2,1,1,64,640]{5,4,3,2,1,0:T(8,128)(2,1)S(1)}, bf16[2,2,1,1,64,640]{5,4,3,2,1,0:T(8,128)(2,1)S(1)}, u32[]{:S(2)}, u32[]{:S(2)}) collective-permute-start(bf16[2,2,1,1,64,640]{5,4,3,2,1,0:T(8,128)(2,1)S(1)} %dynamic-slice_convert_fusion.1), channel_id=1, source_target_pairs={{0,8},{4,12},{8,0},{12,4},{16,24},{20,28},{24,16},{28,20},{1,9},{5... | collective-permute-start | bytes 983048 | tf_op jit(solution)/shard_map/ppermute | solution.py:386
  358.6 21.6 %collective-permute-start.43 = (bf16[1,1,1,64,512]{4,3,2,1,0:T(8,128)(2,1)S(1)}, bf16[1,1,1,64,512]{4,3,2,1,0:T(8,128)(2,1)S(1)}, u32[]{:S(2)}, u32[]{:S(2)}) collective-permute-start(bf16[1,1,1,64,512]{4,3,2,1,0:T(8,128)(2,1)S(1)} %dynamic-slice_convert_fusion.7), channel_id=1, source_target_pairs={{0,16},{4,20},{8,24},{12,28},{16,0},{20,4},{24,8},{28,12},{1,17},{... | collective-permute-start | bytes 196616 | tf_op jit(solution)/shard_map/ppermute | solution.py:386
  363.2 22.6 %collective-permute-start.21 = (bf16[2,1,2,392,512]{4,3,2,1,0:T(8,128)(2,1)S(1)}, bf16[2,1,2,392,512]{4,3,2,1,0:T(8,128)(2,1)S(1)}, u32[]{:S(2)}, u32[]{:S(2)}) collective-permute-start(bf16[2,1,2,392,512]{4,3,2,1,0:T(8,128)(2,1)S(1)} %pad_maximum_fusion.4), channel_id=1, source_target_pairs={{0,1},{1,0},{2,3},{3,2},{4,5},{5,4},{6,7},{7,6},{8,9},{9,8},{10,11... | collective-permute-start | bytes 4816904 | tf_op jit(solution)/shard_map/ppermute | solution.py:386
  364.9 14.7 %collective-permute-start.37 = (bf16[2,1,1,1,64,640]{5,4,3,2,1,0:T(8,128)(2,1)S(1)}, bf16[2,1,1,1,64,640]{5,4,3,2,1,0:T(8,128)(2,1)S(1)}, u32[]{:S(2)}, u32[]{:S(2)}) collective-permute-start(bf16[2,1,1,1,64,640]{5,4,3,2,1,0:T(8,128)(2,1)S(1)} %dynamic-slice_convert_fusion.4), channel_id=1, source_target_pairs={{0,16},{4,20},{8,24},{12,28},{16,0},{20,4},{24,8},{28,12},{1,17},{... | collective-permute-start | bytes 491528 | tf_op jit(solution)/shard_map/ppermute | solution.py:386
  379.5 10.7 %collective-permute-start.19 = (bf16[2,1,2,392,512]{4,3,2,1,0:T(8,128)(2,1)S(1)}, bf16[2,1,2,392,512]{4,3,2,1,0:T(8,128)(2,1)S(1)}, u32[]{:S(2)}, u32[]{:S(2)}) collective-permute-start(bf16[2,1,2,392,512]{4,3,2,1,0:T(8,128)(2,1)S(1)} %pad_maximum_fusion.3), channel_id=1, source_target_pairs={{0,1},{1,0},{2,3},{3,2},{4,5},{5,4},{6,7},{7,6},{8,9},{9,8},{10,11... | collective-permute-start | bytes 4816904 | tf_op jit(solution)/shard_map/ppermute | solution.py:386
  379.7 4.9 %collective-permute-start.38 = (bf16[1,1,1,64,640]{4,3,2,1,0:T(8,128)(2,1)S(1)}, bf16[1,1,1,64,640]{4,3,2,1,0:T(8,128)(2,1)S(1)}, u32[]{:S(2)}, u32[]{:S(2)}) collective-permute-start(bf16[1,1,1,64,640]{4,3,2,1,0:T(8,128)(2,1)S(1)} %fusion.24), channel_id=1, source_target_pairs={{0,2},{1,3},{2,0},{3,1},{4,6},{5,7},{6,4},{7,5},{8,10},{9,11},{10,... | collective-permute-start | bytes 245768 | tf_op jit(solution)/shard_map/ppermute | solution.py:386
  (32 other events, 258.1 us)
